TPU v7x, 256 devices: a whole 4x4x8 slice. The times are simulated.
256 devices in a mesh: sx: 8 (over z), sy: 16 (over y, x_hi, core), grp: 2 (over x_lo).
Axes of the slice: x: 4 (x_hi: 2, x_lo: 2; x = x_hi * 2 + x_lo), y: 4, z: 8, core: 2. Of those that a mesh axis runs over, the one named last changes fastest.
Arguments:
- velocity: float32 [3, 16, 256, 2048], P(None, 'grp', 'sx', 'sy'), may hold values from -6 to 6
- target_stress: float32 [6, 16, 256, 2048], P(None, 'grp', 'sx', 'sy'), may hold values from -6 to 6
- w_conv: bfloat16 [27, 128], replicated, may hold values from -1.25 to 1.25
- b_conv: float32 [128], replicated, may hold values from -3 to 3
- w_mix: bfloat16 [128, 128], replicated, may hold values from -0.5 to 0.5
- b_mix: float32 [128], replicated, may hold values from -3 to 3
- w_out: bfloat16 [128, 6], replicated, may hold values from -0.5 to 0.5
- plane_offsets: int32 [2, 8, 16, 2], P('grp', 'sx', 'sy'), may hold values from 0 to 7
- trainer_map: int32 [2, 8, 32, 1], P('grp', 'sx'), may hold values from 0 to 15; in each aligned block of 32 rows (0 to 31, 32 to 63, ..., all dimensions but the last counted through in order) at most 4 rows name the same one
Outputs:
- tendency: float32 [3, 16, 256, 2048], P(None, 'grp', 'sx', 'sy')
- grad_conv: float32 [27, 128], replicated
- grad_bconv: float32 [128], replicated
- grad_mix: float32 [128, 128], replicated
- grad_bmix: float32 [128], replicated
- grad_out: float32 [128, 6], replicated
Inputs may be any that keep to these rules, and one draw needn't show every extreme that they name: `trainer_map`: within one row of tiles (one index of grp and sx) no trainer index is named by more than 4 samples, a bound that some block reaches.
All inputs are finite; a program needn't handle non-finite values.
Results may differ from a plain program's by a relative error of at most 0.004.
Values sent between devices are 32-bit elements; how exact they have to be, the bound alone decides.
A program may use at most 64 MiB of HBM per device.

v0:
```python
import math

import jax
import jax.numpy as jnp
from jax import lax
from jax.sharding import PartitionSpec as P

S = 2


gelu_c = 0.7978845608
gelu_k = 0.044715
visc = 0.1


def with_halo(cells, sides, width):
    for axis, dim in sides:
        count = lax.axis_size(axis)
        head = lax.slice_in_dim(cells, 0, width, axis=dim)
        tail = lax.slice_in_dim(cells, cells.shape[dim] - width, cells.shape[dim], axis=dim)
        cells = jnp.concatenate(
            [
                lax.ppermute(tail, axis, [(i, (i + 1) % count) for i in range(count)]),
                cells,
                lax.ppermute(head, axis, [((i + 1) % count, i) for i in range(count)]),
            ],
            axis=dim,
        )
    return cells


def gelu_value(v):
    return 0.5 * v * (1.0 + jnp.tanh(gelu_c * (v + gelu_k * v * v * v)))


def gelu_slope(v):
    tval = jnp.tanh(gelu_c * (v + gelu_k * v * v * v))
    return 0.5 * (1.0 + tval) + 0.5 * v * (1.0 - tval * tval) * gelu_c * (
        1.0 + 3.0 * gelu_k * v * v
    )


def patches(plane, width_x, width_y):
    parts = [plane[:, a : a + width_x, b : b + width_y] for a in range(3) for b in range(3)]
    return jnp.stack(parts, axis=1).reshape(27, width_x * width_y)


def forward(pats, w_conv, b_conv, w_mix, b_mix, w_out):
    pre_one = (
        lax.dot_general(pats, w_conv, (((0,), (0,)), ((), ())), preferred_element_type=jnp.float32)
        + b_conv
    )
    hidden_one = gelu_value(pre_one).astype(jnp.bfloat16)
    pre_two = jnp.dot(hidden_one, w_mix, preferred_element_type=jnp.float32) + b_mix
    hidden_two = gelu_value(pre_two).astype(jnp.bfloat16)
    stress = lax.dot_general(
        w_out, hidden_two, (((0,), (1,)), ((), ())), preferred_element_type=jnp.float32
    )
    return (pre_one, hidden_one, pre_two, hidden_two, stress)


def train_grads(pats, target, scale, w_conv, b_conv, w_mix, b_mix, w_out):
    pre_one, hidden_one, pre_two, hidden_two, stress = forward(
        pats, w_conv, b_conv, w_mix, b_mix, w_out
    )
    errors = ((stress - target) * scale).astype(jnp.bfloat16)
    g_out = lax.dot_general(
        hidden_two, errors, (((0,), (1,)), ((), ())), preferred_element_type=jnp.float32
    )
    back_two = lax.dot_general(
        errors, w_out, (((0,), (1,)), ((), ())), preferred_element_type=jnp.float32
    )
    delta_two = (back_two * gelu_slope(pre_two)).astype(jnp.bfloat16)
    g_bmix = jnp.sum(delta_two, axis=0, dtype=jnp.float32)
    g_mix = lax.dot_general(
        hidden_one, delta_two, (((0,), (0,)), ((), ())), preferred_element_type=jnp.float32
    )
    back_one = lax.dot_general(
        delta_two, w_mix, (((1,), (1,)), ((), ())), preferred_element_type=jnp.float32
    )
    delta_one = (back_one * gelu_slope(pre_one)).astype(jnp.bfloat16)
    g_bconv = jnp.sum(delta_one, axis=0, dtype=jnp.float32)
    g_conv = lax.dot_general(
        pats, delta_one, (((1,), (0,)), ((), ())), preferred_element_type=jnp.float32
    )
    return (g_conv, g_bconv, g_mix, g_bmix, g_out)


def closure(field_b, width_x, width_y, weights):

    def infer(plane):
        return forward(patches(plane, width_x, width_y), *weights)[4].reshape(6, width_x, width_y)

    return jnp.transpose(lax.map(infer, jnp.transpose(field_b, (1, 0, 2, 3))), (1, 0, 2, 3))


def shifted(array, step_z, step_x, step_y):
    depth, rows, cols = (array.shape[1], array.shape[2], array.shape[3])
    return array[
        :,
        1 + step_z : depth - 1 + step_z,
        1 + step_x : rows - 1 + step_x,
        1 + step_y : cols - 1 + step_y,
    ]


def rates(padded, stress_pad):
    lap = -6.0 * shifted(padded, 0, 0, 0)
    for step in (1, -1):
        lap = (
            lap
            + shifted(padded, step, 0, 0)
            + shifted(padded, 0, step, 0)
            + shifted(padded, 0, 0, step)
        )
    along_x = 0.5 * (shifted(stress_pad, 0, 1, 0) - shifted(stress_pad, 0, -1, 0))
    along_y = 0.5 * (shifted(stress_pad, 0, 0, 1) - shifted(stress_pad, 0, 0, -1))
    along_z = 0.5 * (shifted(stress_pad, 1, 0, 0) - shifted(stress_pad, -1, 0, 0))
    force_x = along_x[0] + along_y[3] + along_z[4]
    force_y = along_x[3] + along_y[1] + along_z[5]
    force_z = along_x[4] + along_y[5] + along_z[2]
    return jnp.stack([visc * lap[0] - force_x, visc * lap[1] - force_y, visc * lap[2] - force_z])


def batch_grads(planes, targets, scales, weights):
    count_slots, width_x, width_y = (planes.shape[0], planes.shape[2], planes.shape[3])
    cells = width_x * width_y
    padded = jnp.pad(planes, ((0, 0), (0, 0), (1, 1), (1, 1)))
    pats = jnp.concatenate(
        [patches(padded[slot], width_x, width_y) for slot in range(count_slots)], axis=1
    )
    target = jnp.transpose(targets, (1, 0, 2, 3)).reshape(6, count_slots * cells)
    scale_cells = jnp.repeat(scales, cells)[None, :]
    return train_grads(pats, target, scale_cells, *weights)


def shards(
    velocity, target_stress, w_conv, b_conv, w_mix, b_mix, w_out, plane_offsets, trainer_map
):
    weights = (w_conv, b_conv, w_mix, b_mix, w_out)
    width_x, width_y = (velocity.shape[2], velocity.shape[3])
    padded = with_halo(velocity, (("sx", 2), ("sy", 3), ("grp", 1)), 1)
    stress = closure(padded[:, 1:-1].astype(jnp.bfloat16), width_x, width_y, weights)
    stress_pad = with_halo(stress, (("sx", 2), ("sy", 3), ("grp", 1)), 1)
    tendency = rates(padded, stress_pad)
    total_samples = S * lax.axis_size("sx") * lax.axis_size("sy") * lax.axis_size("grp")
    gscale = 1.0 / math.sqrt(total_samples * width_x * width_y)
    mine = lax.axis_index("sy")
    row = trainer_map[0, 0, :, 0]
    offsets = plane_offsets[0, 0, 0, :]
    own_planes = jnp.transpose(
        jnp.take(velocity.astype(jnp.bfloat16), offsets, axis=1), (1, 0, 2, 3)
    )
    own_targets = jnp.transpose(jnp.take(target_stress, offsets, axis=1), (1, 0, 2, 3))
    destinations = lax.dynamic_slice_in_dim(row, mine * S, S)
    counts = jnp.sum((row[None, :] == destinations[:, None]).astype(jnp.float32), axis=1)
    scales = 2.0 * gscale / counts
    grads = batch_grads(own_planes, own_targets, scales, weights)
    summed = lax.psum((grads[0], grads[1], grads[2], grads[3], grads[4]), ("sx", "sy", "grp"))
    return (tendency, summed[0], summed[1], summed[2], summed[3], summed[4])


def solution(mesh):
    in_specs = (
        P(None, "grp", "sx", "sy"),
        P(None, "grp", "sx", "sy"),
        P(),
        P(),
        P(),
        P(),
        P(),
        P("grp", "sx", "sy", None),
        P("grp", "sx", None, None),
    )
    out_specs = (P(None, "grp", "sx", "sy"), P(), P(), P(), P(), P())
    return jax.shard_map(shards, mesh=mesh, in_specs=in_specs, out_specs=out_specs, check_vma=False)
```

profile of v0, /device:TPU:1, one launch (start us, length us, event | category | flops | bytes accessed | tf_op | source)
XLA Modules:
  0.0 275.6 jit_solution(18281357517347173363)
XLA Ops:
  8.6 1.0 convert_element_type.39
  13.0 3.7 %multiply_convert_fusion.1 = (bf16[8192,128]{1,0:T(8,128)(2,1)S(1)}, f32[8192,128]{1,0:T(8,128)}) fusion(f32[128]{0:T(128)S(1)} %copy-done.14, bf16[27,8192]{1,0:T(8,128)(2,1)S(1)} %constant_dynamic-update-slice_fusion.18, bf16[27,128]{1,0:T(8,128)(2,1)S(1)} %copy-done.12), kind=kOutput, calls=%fused_computation.73 | convolution fusion | flops 67108864 | bytes 6741248 | tf_op jit(solution)/shard_map/dot_general | solution.py:50
  16.7 1.7 multiply_convert_fusion
  19.1 3.2 %convert_reduce_fusion = (f32[128]{0:T(128)S(1)}, bf16[8192,128]{1,0:T(8,128)(2,1)S(1)}) fusion(f32[8192,128]{1,0:T(8,128)S(1)} %get-tuple-element.149, bf16[6,8192]{1,0:T(8,128)(2,1)S(1)} %fusion.32, bf16[128,6]{0,1:T(8,128)(2,1)S(1)} %copy-done.10), kind=kOutput, calls=%fused_computation.70 | convolution fusion | flops 34602880 | bytes 6391808 | tf_op jit(solution)/shard_map/dot_general | solution.py:70
  22.3 1.4 copy-done.4
  23.7 1.4 fusion.67
  25.1 2.5 collective-permute-start
  27.7 4.2 %collective-permute-start.1 = (f32[3,8,1,128]{3,1,2,0:T(8,128)S(1)}, f32[3,8,1,128]{3,1,2,0:T(8,128)S(1)}, u32[]{:S(2)}, u32[]{:S(2)}) collective-permute-start(f32[3,8,1,128]{3,1,2,0:T(8,128)S(1)} %bitcast.275), channel_id=1, source_target_pairs={{32,0},{64,32},{96,64},{128,96},{160,128},{192,160},{224,192},{0,2... | collective-permute-start | bytes 36872 | tf_op jit(solution)/shard_map/ppermute | solution.py:25
  31.9 5.8 %convert_reduce_fusion.1 = (f32[128]{0:T(128)S(1)}, bf16[8192,128]{1,0:T(8,128)(2,1)S(1)}) fusion(f32[8192,128]{1,0:T(8,128)} %get-tuple-element.147, bf16[8192,128]{1,0:T(8,128)(2,1)} %copy-done.4, bf16[128,128]{1,0:T(8,128)(2,1)S(1)} %copy-done.11), kind=kOutput, calls=%fused_computation.71 | convolution fusion | flops 290455424 | bytes 8421888 | tf_op jit(solution)/shard_map/dot_general | solution.py:78
  38.8 3.7 %collective-permute-start.2 = (f32[3,8,34,1]{3,2,1,0:T(8,128)S(1)}, f32[3,8,34,1]{3,2,1,0:T(8,128)S(1)}, u32[]{:S(2)}, u32[]{:S(2)}) collective-permute-start(f32[3,8,34,1]{3,2,1,0:T(8,128)S(1)} %get-tuple-element.140), channel_id=1, source_target_pairs={{0,2},{2,4},{4,6},{6,8},{8,10},{10,12},{12,14},{14,16},{16,18},{18... | collective-permute-start | bytes 9800 | tf_op jit(solution)/shard_map/ppermute | solution.py:23
  42.5 80.8 %all-reduce.1 = (f32[27,128]{1,0:T(8,128)}, f32[128]{0:T(128)}, f32[128]{0:T(128)}, f32[128,6]{0,1:T(8,128)}) all-reduce(f32[27,128]{1,0:T(8,128)S(1)} %fusion.66, f32[128]{0:T(128)S(1)} %get-tuple-element.150, f32[128]{0:T(128)S(1)} %get-tuple-element.152, ...), channel_id=1, replica_groups=mesh['sx'=8,'sy'=16,'grp'=2] {'sx','sy','grp'}, use_global_device_ids=true, to_apply=%region_3.4 | all-reduce | flops 4480 | bytes 35840 | tf_op jit(solution)/shard_map/psum | solution.py:159
  123.3 1.3 convert_bitcast_fusion
  124.6 60.2 %while.10 = (s32[]{:T(128)}, f32[8,6,32,128]{3,0,2,1:T(8,128)}, bf16[8,3,34,130]{3,2,0,1:T(8,128)(2,1)}, bf16[27,128]{1,0:T(8,128)(2,1)S(1)}, f32[128]{0:T(128)S...) while((s32[]{:T(128)}, f32[8,6,32,128]{3,0,2,1:T(8,128)}, ...), condition=%wide.region_1.2_spmd, body=%wide.region_0.1_spmd.sunk | while | flops 179306496 | bytes 4355239 | solution.py:94
  124.6 0.8 dynamic-slice_bitcast_fusion.3
  126.2 1.7 fusion.119
  128.3 3.8 %dynamic_update_slice.5 = f32[8,6,32,128]{3,0,2,1:T(8,128)} dynamic-update-slice(f32[8,6,32,128]{3,0,2,1:T(8,128)} %get-tuple-element.217, f32[1,6,32,128]{3,0,2,1:T(1,128)S(1)} %bitcast.253, s32[]{:T(128)} %get-tuple-element.216, s32[]{:T(128)} %constant.35.clone.1..sunk, s32[]{:T(128)} %constant.35.clone.1..sunk, s32[]{:T(128)} %constant.35.clone.1..sunk) | dynamic-update-slice | bytes 196612 | tf_op jit(solution)/shard_map/while/body/jit(dynamic_update_index_in_dim)/dynamic_update_slice | solution.py:94
  133.8 1.7 fusion.119
  135.9 3.8 %dynamic_update_slice.5 = f32[8,6,32,128]{3,0,2,1:T(8,128)} dynamic-update-slice(f32[8,6,32,128]{3,0,2,1:T(8,128)} %get-tuple-element.217, f32[1,6,32,128]{3,0,2,1:T(1,128)S(1)} %bitcast.253, s32[]{:T(128)} %get-tuple-element.216, s32[]{:T(128)} %constant.35.clone.1..sunk, s32[]{:T(128)} %constant.35.clone.1..sunk, s32[]{:T(128)} %constant.35.clone.1..sunk) | dynamic-update-slice | bytes 196612 | tf_op jit(solution)/shard_map/while/body/jit(dynamic_update_index_in_dim)/dynamic_update_slice | solution.py:94
  141.3 1.7 fusion.119
  143.4 3.8 %dynamic_update_slice.5 = f32[8,6,32,128]{3,0,2,1:T(8,128)} dynamic-update-slice(f32[8,6,32,128]{3,0,2,1:T(8,128)} %get-tuple-element.217, f32[1,6,32,128]{3,0,2,1:T(1,128)S(1)} %bitcast.253, s32[]{:T(128)} %get-tuple-element.216, s32[]{:T(128)} %constant.35.clone.1..sunk, s32[]{:T(128)} %constant.35.clone.1..sunk, s32[]{:T(128)} %constant.35.clone.1..sunk) | dynamic-update-slice | bytes 196612 | tf_op jit(solution)/shard_map/while/body/jit(dynamic_update_index_in_dim)/dynamic_update_slice | solution.py:94
  148.8 1.7 fusion.119
  150.9 3.8 %dynamic_update_slice.5 = f32[8,6,32,128]{3,0,2,1:T(8,128)} dynamic-update-slice(f32[8,6,32,128]{3,0,2,1:T(8,128)} %get-tuple-element.217, f32[1,6,32,128]{3,0,2,1:T(1,128)S(1)} %bitcast.253, s32[]{:T(128)} %get-tuple-element.216, s32[]{:T(128)} %constant.35.clone.1..sunk, s32[]{:T(128)} %constant.35.clone.1..sunk, s32[]{:T(128)} %constant.35.clone.1..sunk) | dynamic-update-slice | bytes 196612 | tf_op jit(solution)/shard_map/while/body/jit(dynamic_update_index_in_dim)/dynamic_update_slice | solution.py:94
  156.3 1.7 fusion.119
  158.4 3.8 %dynamic_update_slice.5 = f32[8,6,32,128]{3,0,2,1:T(8,128)} dynamic-update-slice(f32[8,6,32,128]{3,0,2,1:T(8,128)} %get-tuple-element.217, f32[1,6,32,128]{3,0,2,1:T(1,128)S(1)} %bitcast.253, s32[]{:T(128)} %get-tuple-element.216, s32[]{:T(128)} %constant.35.clone.1..sunk, s32[]{:T(128)} %constant.35.clone.1..sunk, s32[]{:T(128)} %constant.35.clone.1..sunk) | dynamic-update-slice | bytes 196612 | tf_op jit(solution)/shard_map/while/body/jit(dynamic_update_index_in_dim)/dynamic_update_slice | solution.py:94
  163.9 1.7 fusion.119
  166.0 3.8 %dynamic_update_slice.5 = f32[8,6,32,128]{3,0,2,1:T(8,128)} dynamic-update-slice(f32[8,6,32,128]{3,0,2,1:T(8,128)} %get-tuple-element.217, f32[1,6,32,128]{3,0,2,1:T(1,128)S(1)} %bitcast.253, s32[]{:T(128)} %get-tuple-element.216, s32[]{:T(128)} %constant.35.clone.1..sunk, s32[]{:T(128)} %constant.35.clone.1..sunk, s32[]{:T(128)} %constant.35.clone.1..sunk) | dynamic-update-slice | bytes 196612 | tf_op jit(solution)/shard_map/while/body/jit(dynamic_update_index_in_dim)/dynamic_update_slice | solution.py:94
  169.8 0.8 dynamic-slice_bitcast_fusion.3
  171.4 1.7 fusion.119
  173.5 3.8 %dynamic_update_slice.5 = f32[8,6,32,128]{3,0,2,1:T(8,128)} dynamic-update-slice(f32[8,6,32,128]{3,0,2,1:T(8,128)} %get-tuple-element.217, f32[1,6,32,128]{3,0,2,1:T(1,128)S(1)} %bitcast.253, s32[]{:T(128)} %get-tuple-element.216, s32[]{:T(128)} %constant.35.clone.1..sunk, s32[]{:T(128)} %constant.35.clone.1..sunk, s32[]{:T(128)} %constant.35.clone.1..sunk) | dynamic-update-slice | bytes 196612 | tf_op jit(solution)/shard_map/while/body/jit(dynamic_update_index_in_dim)/dynamic_update_slice | solution.py:94
  178.9 1.7 fusion.119
  181.0 3.8 %dynamic_update_slice.5 = f32[8,6,32,128]{3,0,2,1:T(8,128)} dynamic-update-slice(f32[8,6,32,128]{3,0,2,1:T(8,128)} %get-tuple-element.217, f32[1,6,32,128]{3,0,2,1:T(1,128)S(1)} %bitcast.253, s32[]{:T(128)} %get-tuple-element.216, s32[]{:T(128)} %constant.35.clone.1..sunk, s32[]{:T(128)} %constant.35.clone.1..sunk, s32[]{:T(128)} %constant.35.clone.1..sunk) | dynamic-update-slice | bytes 196612 | tf_op jit(solution)/shard_map/while/body/jit(dynamic_update_index_in_dim)/dynamic_update_slice | solution.py:94
  189.3 0.9 collective-permute-done.7
  190.2 1.2 pad_maximum_fusion.1
  191.4 1.4 fusion.62
  192.8 1.6 copy.158
  194.4 2.2 collective-permute-start.8
  196.6 1.6 copy.159
  198.2 1.2 collective-permute-start.9
  199.5 1.2 fusion.47
  201.3 1.4 copy.143
  202.7 1.3 pad_maximum_fusion.34
  204.0 1.2 collective-permute-start.10
  205.6 2.1 fusion.48
  207.7 1.5 collective-permute-done.10
  209.2 3.8 %collective-permute-done.11 = f32[6,1,34,130]{3,2,1,0:T(8,128)S(1)} collective-permute-done((f32[6,1,34,130]{3,2,1,0:T(8,128)S(1)}, f32[6,1,34,130]{3,2,1,0:T(8,128)S(1)}, u32[]{:S(2)}, u32[]{:S(2)}) %collective-permute-start.11) | collective-permute-done | bytes 106112 | tf_op jit(solution)/shard_map/ppermute | solution.py:23
  213.0 1.1 fusion.46
  215.0 52.2 %all-reduce.4.cloned.1.call-done = f32[128,128]{1,0:T(8,128)} async-done(((f32[128,128]{1,0:T(8,128)}), f32[128,128]{1,0:T(8,128)}) %all-reduce.4.cloned.1.call-update) | async-done | bytes 65552 | tf_op jit(solution)/shard_map/psum | solution.py:159
  267.2 1.5 copy.213
  (211 shorter events, 27.1 us)
Async XLA Ops:
  7.2 5.2 %copy-start = (f32[6,8,32,128]{3,2,1,0:T(8,128)S(1)}, f32[6,8,32,128]{3,2,1,0:T(8,128)}, u32[]{:S(2)}) copy-start(f32[6,8,32,128]{3,2,1,0:T(8,128)} %param.12) | copy-start | bytes 2359300
  7.2 4.8 %copy-start.13 = (s32[1,1,32,1]{2,3,1,0:T(1,128)S(1)}, s32[1,1,32,1]{2,3,1,0:T(1,128)}, u32[]{:S(2)}) copy-start(s32[1,1,32,1]{2,3,1,0:T(1,128)} %param.19) | copy-start | bytes 388
  7.2 5.8 %copy-start.12 = (bf16[27,128]{1,0:T(8,128)(2,1)S(1)}, bf16[27,128]{1,0:T(8,128)(2,1)}, u32[]{:S(2)}) copy-start(bf16[27,128]{1,0:T(8,128)(2,1)} %param.13) | copy-start | bytes 20740
  7.2 5.8 %copy-start.14 = (f32[128]{0:T(128)S(1)}, f32[128]{0:T(128)}, u32[]{:S(2)}) copy-start(f32[128]{0:T(128)} %param.14) | copy-start | bytes 1540
  7.2 260.0 %all-reduce.4.cloned.1.call-start = ((), (), s32[]{:S(2)}) async-start(), calls=%async_computation | async-start | bytes 131072 | tf_op jit(solution)/shard_map/psum | solution.py:159
  13.0 3.7 %copy-start.8 = (bf16[27,8192]{1,0:T(8,128)(2,1)}, bf16[27,8192]{1,0:T(8,128)(2,1)S(1)}, u32[]{:S(2)}) copy-start(bf16[27,8192]{1,0:T(8,128)(2,1)S(1)} %constant_dynamic-update-slice_fusion.18) | copy-start | bytes 1327108
  13.0 3.7 %copy-start.11 = (bf16[128,128]{1,0:T(8,128)(2,1)S(1)}, bf16[128,128]{1,0:T(8,128)(2,1)}, u32[]{:S(2)}) copy-start(bf16[128,128]{1,0:T(8,128)(2,1)} %param.15) | copy-start | bytes 98308
  13.0 3.7 %copy-start.15 = (f32[128]{0:T(128)S(1)}, f32[128]{0:T(128)}, u32[]{:S(2)}) copy-start(f32[128]{0:T(128)} %param.16) | copy-start | bytes 1540
  16.7 1.8 copy-start.10
  22.3 1.4 copy-start.4
  22.3 2.8 %copy-start.2 = (f32[3,8,32,128]{3,2,1,0:T(8,128)S(1)}, f32[3,8,32,128]{3,2,1,0:T(8,128)}, u32[]{:S(2)}) copy-start(f32[3,8,32,128]{3,2,1,0:T(8,128)} %param.11) | copy-start | bytes 1179652
  25.1 13.4 %collective-permute-start = (f32[3,8,1,128]{3,1,2,0:T(8,128)S(1)}, f32[3,8,1,128]{3,1,2,0:T(8,128)S(1)}, u32[]{:S(2)}, u32[]{:S(2)}) collective-permute-start(f32[3,8,1,128]{3,1,2,0:T(8,128)S(1)} %bitcast.276), channel_id=1, source_target_pairs={{0,32},{32,64},{64,96},{96,128},{128,160},{160,192},{192,224},{224... | collective-permute-start | bytes 36872 | tf_op jit(solution)/shard_map/ppermute | solution.py:23
  27.7 10.9 %collective-permute-start.1 = (f32[3,8,1,128]{3,1,2,0:T(8,128)S(1)}, f32[3,8,1,128]{3,1,2,0:T(8,128)S(1)}, u32[]{:S(2)}, u32[]{:S(2)}) collective-permute-start(f32[3,8,1,128]{3,1,2,0:T(8,128)S(1)} %bitcast.275), channel_id=1, source_target_pairs={{32,0},{64,32},{96,64},{128,96},{160,128},{192,160},{224,192},{0,2... | collective-permute-start | bytes 36872 | tf_op jit(solution)/shard_map/ppermute | solution.py:25
  31.9 5.8 %copy-start.9 = (bf16[27,8192]{1,0:T(8,128)(2,1)S(1)}, bf16[27,8192]{1,0:T(8,128)(2,1)}, u32[]{:S(2)}) copy-start(bf16[27,8192]{1,0:T(8,128)(2,1)} %copy-done.8) | copy-start | bytes 1327108
  38.8 84.5 %collective-permute-start.2 = (f32[3,8,34,1]{3,2,1,0:T(8,128)S(1)}, f32[3,8,34,1]{3,2,1,0:T(8,128)S(1)}, u32[]{:S(2)}, u32[]{:S(2)}) collective-permute-start(f32[3,8,34,1]{3,2,1,0:T(8,128)S(1)} %get-tuple-element.140), channel_id=1, source_target_pairs={{0,2},{2,4},{4,6},{6,8},{8,10},{10,12},{12,14},{14,16},{16,18},{18... | collective-permute-start | bytes 9800 | tf_op jit(solution)/shard_map/ppermute | solution.py:23
  42.5 80.8 %collective-permute-start.3 = (f32[3,8,34,1]{3,2,1,0:T(8,128)S(1)}, f32[3,8,34,1]{3,2,1,0:T(8,128)S(1)}, u32[]{:S(2)}, u32[]{:S(2)}) collective-permute-start(f32[3,8,34,1]{3,2,1,0:T(8,128)S(1)} %get-tuple-element.141), channel_id=1, source_target_pairs={{2,0},{4,2},{6,4},{8,6},{10,8},{12,10},{14,12},{16,14},{18,16},{20... | collective-permute-start | bytes 9800 | tf_op jit(solution)/shard_map/ppermute | solution.py:25
  123.3 1.4 copy-start.5
  123.3 1.3 copy-start.6
  184.8 14.5 %copy-start.3 = (f32[8,6,32,128]{3,0,2,1:T(8,128)S(1)}, f32[8,6,32,128]{3,0,2,1:T(8,128)}, u32[]{:S(2)}) copy-start(f32[8,6,32,128]{3,0,2,1:T(8,128)} %get-tuple-element.48) | copy-start | bytes 2359300
  185.7 3.7 %collective-permute-start.6 = (f32[6,8,1,128]{3,1,2,0:T(8,128)S(1)}, f32[6,8,1,128]{3,1,2,0:T(8,128)S(1)}, u32[]{:S(2)}, u32[]{:S(2)}) collective-permute-start(f32[6,8,1,128]{3,1,2,0:T(8,128)S(1)} %get-tuple-element.139), channel_id=1, source_target_pairs={{32,0},{64,32},{96,64},{128,96},{160,128},{192,160},{224,192},{0,2... | collective-permute-start | bytes 73736 | tf_op jit(solution)/shard_map/ppermute | solution.py:25
  186.3 3.9 %collective-permute-start.7 = (f32[6,8,1,128]{3,1,2,0:T(8,128)S(1)}, f32[6,8,1,128]{3,1,2,0:T(8,128)S(1)}, u32[]{:S(2)}, u32[]{:S(2)}) collective-permute-start(f32[6,8,1,128]{3,1,2,0:T(8,128)S(1)} %get-tuple-element.138), channel_id=1, source_target_pairs={{0,32},{32,64},{64,96},{96,128},{128,160},{160,192},{192,224},{224... | collective-permute-start | bytes 73736 | tf_op jit(solution)/shard_map/ppermute | solution.py:23
  187.9 17.7 %collective-permute-start.4 = (f32[3,1,34,130]{3,2,1,0:T(8,128)}, f32[3,1,34,130]{3,2,1,0:T(8,128)S(1)}, u32[]{:S(2)}, u32[]{:S(2)}) collective-permute-start(f32[3,1,34,130]{3,2,1,0:T(8,128)} %get-tuple-element.132), channel_id=1, source_target_pairs={{1,0},{0,1},{3,2},{2,3},{5,4},{4,5},{7,6},{6,7},{9,8},{8,9},{11,10... | collective-permute-start | bytes 159128 | tf_op jit(solution)/shard_map/ppermute | solution.py:25
  188.7 16.9 %collective-permute-start.5 = (f32[3,1,34,130]{3,2,1,0:T(8,128)}, f32[3,1,34,130]{3,2,1,0:T(8,128)S(1)}, u32[]{:S(2)}, u32[]{:S(2)}) collective-permute-start(f32[3,1,34,130]{3,2,1,0:T(8,128)} %get-tuple-element.133), channel_id=1, source_target_pairs={{0,1},{1,0},{2,3},{3,2},{4,5},{5,4},{6,7},{7,6},{8,9},{9,8},{10,11... | collective-permute-start | bytes 159128 | tf_op jit(solution)/shard_map/ppermute | solution.py:23
  194.4 6.4 %collective-permute-start.8 = (f32[6,8,34,1]{2,1,3,0:T(8,128)S(1)}, f32[6,8,34,1]{2,1,3,0:T(8,128)S(1)}, u32[]{:S(2)}, u32[]{:S(2)}) collective-permute-start(f32[6,8,34,1]{2,1,3,0:T(8,128)S(1)} %copy.158), channel_id=1, source_target_pairs={{2,0},{4,2},{6,4},{8,6},{10,8},{12,10},{14,12},{16,14},{18,16},{20... | collective-permute-start | bytes 19592 | tf_op jit(solution)/shard_map/ppermute | solution.py:25
  198.2 3.1 %collective-permute-start.9 = (f32[6,8,34,1]{2,1,3,0:T(8,128)S(1)}, f32[6,8,34,1]{2,1,3,0:T(8,128)S(1)}, u32[]{:S(2)}, u32[]{:S(2)}) collective-permute-start(f32[6,8,34,1]{2,1,3,0:T(8,128)S(1)} %copy.159), channel_id=1, source_target_pairs={{0,2},{2,4},{4,6},{6,8},{8,10},{10,12},{12,14},{14,16},{16,18},{18... | collective-permute-start | bytes 19592 | tf_op jit(solution)/shard_map/ppermute | solution.py:23
  202.7 10.3 %copy-start.1 = (f32[6,8,34,1]{3,2,1,0:T(8,128)S(1)}, f32[6,8,34,1]{3,2,1,0:T(8,128)}, u32[]{:S(2)}) copy-start(f32[6,8,34,1]{3,2,1,0:T(8,128)} %copy.143) | copy-start | bytes 19588
  204.0 10.1 %copy-start.7 = (f32[6,8,32,128]{3,2,1,0:T(8,128)S(1)}, f32[6,8,32,128]{3,2,1,0:T(8,128)}, u32[]{:S(2)}) copy-start(f32[6,8,32,128]{3,2,1,0:T(8,128)} %fusion.47) | copy-start | bytes 2359300
  204.0 5.2 %collective-permute-start.10 = (f32[6,1,34,130]{3,2,1,0:T(8,128)S(1)}, f32[6,1,34,130]{3,2,1,0:T(8,128)S(1)}, u32[]{:S(2)}, u32[]{:S(2)}) collective-permute-start(f32[6,1,34,130]{3,2,1,0:T(8,128)S(1)} %get-tuple-element.127), channel_id=1, source_target_pairs={{1,0},{0,1},{3,2},{2,3},{5,4},{4,5},{7,6},{6,7},{9,8},{8,9},{11,10... | collective-permute-start | bytes 318248 | tf_op jit(solution)/shard_map/ppermute | solution.py:25
  205.2 7.7 %collective-permute-start.11 = (f32[6,1,34,130]{3,2,1,0:T(8,128)S(1)}, f32[6,1,34,130]{3,2,1,0:T(8,128)S(1)}, u32[]{:S(2)}, u32[]{:S(2)}) collective-permute-start(f32[6,1,34,130]{3,2,1,0:T(8,128)S(1)} %get-tuple-element.128), channel_id=1, source_target_pairs={{0,1},{1,0},{2,3},{3,2},{4,5},{5,4},{6,7},{7,6},{8,9},{9,8},{10,11... | collective-permute-start | bytes 318248 | tf_op jit(solution)/shard_map/ppermute | solution.py:23
Sparse Core Ops, SparseCore 0:
  25.2 241.9 all-reduce.3
where the time goes:
time: 277 us; the launch traced here: 276 us
  blocking collectives  80.8 us (29%)
  waiting for transfers between devices  58.4 us (21%)
  local copies, waits for them, and re-layouts  57.7 us (21%)
  matrix products  33.7 us (12%)
  starting transfers between devices  18.3 us (7%)
  between operations  14.4 us (5%)
  other arithmetic  12 us (4%)
    psum x1, blocking collectives, shards(): lax.psum((grads[0], grads[1], grads[2], grads[3], grads[4]), ('sx', 'sy',...  80.8 us
    psum x1, waiting for transfers between devices, shards(): lax.psum((grads[0], grads[1], grads[2], grads[3], grads[4]), ('sx', 'sy',...  52.2 us
    dynamic_update_slice x8, local copies, waits for them, and re-layouts, closure(): lax.map(infer, jnp.transpose(field_b, (1, 0, 2, 3)))  30.6 us
    dot_general x9, matrix products, forward(): jnp.dot(hidden_one, w_mix, preferred_element_type=jnp.float32) + b_mix  15.1 us
    ppermute x6, starting transfers between devices, with_halo(): lax.ppermute(tail, axis, [(i, (i + 1) % count) for i in range(count)])  9.26 us
    ppermute x6, starting transfers between devices, with_halo(): lax.ppermute(head, axis, [((i + 1) % count, i) for i in range(count)])  9.01 us
    unnamed x58, local copies, waits for them, and re-layouts  7.44 us
    squeeze x8, local copies, waits for them, and re-layouts, closure(): lax.map(infer, jnp.transpose(field_b, (1, 0, 2, 3)))  6.67 us
  transfers between devices with their start and end apart: 13, of which 4 were waited for; matrix products, arithmetic and copies ran while one was open for 31% of the time, Pallas kernels for 0%

commit v1 on v0

v1 whole, which is shorter than its diff:
```python
import functools
import math

import jax
import jax.numpy as jnp
from jax import lax
from jax.experimental import pallas as pl
from jax.experimental.pallas import tpu as pltpu
from jax.sharding import PartitionSpec as P

f32 = jnp.float32
bf16 = jnp.bfloat16
MESH = pl.DeviceIdType.MESH
HIGH = lax.Precision.HIGHEST

S = 2
gelu_c = 0.7978845608
gelu_k = 0.044715
visc = 0.1
lam = (gelu_c * gelu_k) ** (1.0 / 3.0)
shift_c = gelu_c / lam

PZ = 8
CX = 32
CY = 128
BLK = 16
PLANE = (CX + 2) * BLK
TROW = 8
TPLANE = (CX + 2) * TROW
XC = 16
NC = XC * CY
GROWS = 192

DX = (0, 3, 4)
DY = (3, 1, 5)
DZ = (4, 5, 2)


def dot(a, b, precision=None):
    return jnp.dot(a, b, preferred_element_type=f32, precision=precision)


def dot_nt(a, b, precision=None):
    return lax.dot_general(
        a, b, (((1,), (1,)), ((), ())), preferred_element_type=f32, precision=precision
    )


def split(value):
    high = value.astype(bf16).astype(f32)
    return high, value - high


def gate(m):
    return (m * jnp.tanh(m * (m * m + shift_c))).astype(bf16)


def lanes(shape):
    return lax.broadcasted_iota(jnp.int32, shape, 1)


def rows(shape):
    return lax.broadcasted_iota(jnp.int32, shape, 0)


def load_patches(buffer, base, count):
    return jnp.concatenate(
        [
            buffer[pl.ds(pl.multiple_of(base + x * BLK, BLK), 3 * BLK), :]
            for x in range(count)
        ],
        axis=1,
    )


def kernel(
    n_sx, n_sy, n_grp, gscale,
    vel, tgt, wc, bc, wm, bm, wo, offs, tmap,
    tend, gconv, gbconv, gmix, gbmix, gout,
    qf, qb, sf, sb, tg, stress, cw, mw, ow, tw1, tw2, wb2, wbo, prep, prep2,
    q1, q2, lin, grad,
    rowsrc, rowdst, colsrc, coldst, zsrc, zdst, hr, cc,
    srowsrc, srowdst, scolsrc, scoldst, scc,
    gseg, ra, sb_sum, rb, fin, rc,
    hs, hrv, ss, srv, a_s, a_r, b_s, b_r, c_s, c_r,
):
    isx, isy, igr = lax.axis_index("sx"), lax.axis_index("sy"), lax.axis_index("grp")
    up_x, down_x = lax.rem(isx + 1, n_sx), lax.rem(isx + n_sx - 1, n_sx)
    ys = (lax.rem(isy + n_sy - 1, n_sy), isy, lax.rem(isy + 1, n_sy))
    other = 1 - igr
    n_b = n_sx * n_grp
    ib = isx * n_grp + igr

    barrier = pltpu.get_barrier_semaphore()

    def greet(device):
        pl.semaphore_signal(barrier, inc=1, device_id=device, device_id_type=MESH)

    def greet_sy(k, _):
        greet((isx, lax.rem(isy + k, n_sy), igr))
        return 0

    def greet_b(k, _):
        at = lax.rem(ib + k, n_b)
        greet((at // n_grp, isy, lax.rem(at, n_grp)))
        return 0

    lax.fori_loop(1, n_sy, greet_sy, 0)
    lax.fori_loop(1, n_b, greet_b, 0)
    for to_x in (up_x, down_x):
        for to_y in (ys[0], ys[2]):
            greet((to_x, to_y, igr))

    for c in range(3):
        for side, x in ((0, 0), (1, CX - 1)):
            rowsrc[side, 8 * c : 8 * c + 8, :] = vel[pl.ds(c * PZ * CX + x, PZ, stride=CX), :]
        for side, p in ((0, PZ - 1), (1, 0)):
            zsrc[side, c * CX : (c + 1) * CX, :] = vel[pl.ds((c * PZ + p) * CX, CX), :]
    lane = lanes((CX, CY))

    def pack_cols(p, acc):
        for c in range(3):
            j = c * PZ + p
            v = vel[pl.ds(pl.multiple_of(j * CX, CX), CX), :]
            acc = jnp.where(lane // 2 == j, pltpu.roll(v, 2 * j + 1, 1), acc)
        return acc

    colsrc[...] = lax.fori_loop(0, PZ, pack_cols, jnp.zeros((CX, CY), f32))

    pl.semaphore_wait(barrier, (n_sy - 1) + (n_b - 1) + 4)

    def halo_copies():
        out = []
        for d in (-1, 0, 1):
            for side, to_x in ((0, up_x), (1, down_x)):
                slot = 1 - d
                out.append(
                    pltpu.make_async_remote_copy(
                        src_ref=rowsrc.at[1 - side],
                        dst_ref=rowdst.at[side, slot],
                        send_sem=hs.at[side * 3 + slot],
                        recv_sem=hrv.at[side * 3 + slot],
                        device_id=(to_x, ys[1 + d], igr),
                        device_id_type=MESH,
                    )
                )
        for side, to_y in ((0, ys[2]), (1, ys[0])):
            out.append(
                pltpu.make_async_remote_copy(
                    src_ref=colsrc,
                    dst_ref=coldst.at[side],
                    send_sem=hs.at[6 + side],
                    recv_sem=hrv.at[6 + side],
                    device_id=(isx, to_y, igr),
                    device_id_type=MESH,
                )
            )
        for side in (0, 1):
            out.append(
                pltpu.make_async_remote_copy(
                    src_ref=zsrc.at[side],
                    dst_ref=zdst.at[side],
                    send_sem=hs.at[8 + side],
                    recv_sem=hrv.at[8 + side],
                    device_id=(isx, isy, other),
                    device_id_type=MESH,
                )
            )
        return out

    halo = halo_copies()
    for copy in halo:
        copy.start()

    prep[...] = jnp.zeros(prep.shape, f32)
    for c in range(3):
        for a in range(3):
            prep[a * BLK + c * 3 : a * BLK + c * 3 + 3, :] = wc[
                c * 9 + 3 * a : c * 9 + 3 * a + 3, :
            ].astype(f32)
    prep[9:10, :] = bc[...]
    w1 = prep[...][0:48, :]
    w2h = wm[...].astype(f32) * 0.5
    row48 = rows((48, 128))
    high, low = split(w1 * lam)
    pad = jnp.zeros((32, 128), f32)
    cw[...] = jnp.concatenate([high, low, pad], axis=0).T.astype(bf16)
    comp = dot(w1 * lam, w2h, HIGH)
    comp = comp + jnp.where(row48 == 9, lam * bm[...], 0.0)
    comp_high, comp_low = split(comp)
    pick16 = (
        (lanes((6, 16)) == rows((6, 16))) | (lanes((6, 16)) == rows((6, 16)) + 8)
    ).astype(bf16)
    wo16 = dot(wo[...], pick16)
    outl = dot(jnp.concatenate([w2h, comp], axis=0), wo16, HIGH)
    out_high, out_low = split(outl)
    outl = jnp.where(lanes((176, 16)) < 8, out_high, out_low)
    mw[0:128, 0:128] = w2h.T.astype(bf16)
    tail = jnp.concatenate([comp_high, comp_low, pad], axis=0)
    mw[0:128, 128:256] = tail.T.astype(bf16)
    prep2[...] = jnp.zeros(prep2.shape, f32)
    prep2[0:176, 0:16] = outl
    mw[128:144, 0:128] = prep2[0:128, :].T[0:16, :].astype(bf16)
    mw[128:144, 128:256] = prep2[128:256, :].T[0:16, :].astype(bf16)
    pick = (lanes((16, 6)) == rows((16, 6))).astype(bf16)
    ow[...] = dot_nt(pick, wo[...]).astype(bf16)
    half_b1 = 0.5 * bc[...]
    bh, rest = split(half_b1)
    bmid, rest = split(rest)
    t1 = jnp.where(row48 == 9, bh, jnp.where(row48 == 10, bmid, jnp.where(row48 == 11, rest, 0.5 * w1)))
    tw1[...] = jnp.concatenate([t1, pad, pad, pad[0:16]], axis=0).T.astype(bf16)
    half_b2 = 0.5 * bm[...]
    bh, rest = split(half_b2)
    bmid, rest = split(rest)
    row128 = rows((128, 128))
    t2 = jnp.where(row128 == 9, bh, jnp.where(row128 == 10, bmid, jnp.where(row128 == 11, rest, 0.0)))
    tw2[:, 0:128] = w2h.T.astype(bf16)
    tw2[:, 128:256] = t2.T.astype(bf16)
    wb2[...] = w2h.astype(bf16)
    wbo[...] = (0.5 * jnp.where(lanes((128, 16)) < 8, wo16, 0.0)).astype(bf16)

    sf[...] = jnp.ones(sf.shape, f32)
    zero8 = jnp.zeros((8, 128), f32)
    tg[...] = jnp.zeros(tg.shape, f32)
    for s in range(S):
        chosen = lax.broadcasted_iota(jnp.int32, (PZ, CX, CY), 0) == offs[s]

        def plane(ref, c, chosen=chosen):
            stack = ref[c * PZ * CX : (c + 1) * PZ * CX, :].reshape(PZ, CX, CY)
            return jnp.sum(jnp.where(chosen, stack, 0.0), axis=0)

        for side in (0, CX + 1):
            at = s * PLANE + side * BLK
            sf[at : at + 8, :] = zero8
            sf[at + 8 : at + 9, :] = zero8[0:1]
        for c in range(3):
            v = plane(vel, c)
            for b in range(3):
                if b == 0:
                    w = jnp.where(lane == 0, 0.0, pltpu.roll(v, 1, 1))
                elif b == 2:
                    w = jnp.where(lane == CY - 1, 0.0, pltpu.roll(v, CY - 1, 1))
                else:
                    w = v
                sf[pl.ds(s * PLANE + BLK + c * 3 + b, CX, stride=BLK), :] = w
        for c in range(6):
            tg[pl.ds(s * CX * TROW + c, CX, stride=TROW), :] = plane(tgt, c)
    sb[...] = sf[...].astype(bf16)
    grad[...] = jnp.zeros(grad.shape, f32)

    names = tmap[...]
    place = lanes(names.shape)

    def scale_of(s):
        dest = jnp.sum(jnp.where(place == isy * S + s, names, 0), axis=1, keepdims=True)
        count = jnp.sum((names == dest).astype(f32), axis=1, keepdims=True)
        return jnp.broadcast_to(2.0 * gscale / count, (8, 128))

    scales = [scale_of(s) for s in range(S)]

    def train(i, _):
        s = i // (CX // XC)
        part = lax.rem(i, CX // XC)
        scale = jnp.where(s == 0, scales[0], scales[1])
        pats = load_patches(sb, s * PLANE + part * (XC * BLK), XC)
        a1 = dot(tw1[:, 0:48], pats)
        p1 = (8.0 * gelu_c * gelu_k) * (a1 * a1) + 2.0 * gelu_c
        t1 = jnp.tanh(a1 * p1)
        s1 = 1.0 + t1
        h1 = (a1 * s1).astype(bf16)
        d1 = s1 * (1.0 + (1.0 - t1) * (a1 * (3.0 * p1 - 4.0 * gelu_c)))
        h1x = jnp.concatenate([h1, pats[0:16]], axis=0)
        a2 = dot(tw2[:, 0:144], h1x)
        p2 = (8.0 * gelu_c * gelu_k) * (a2 * a2) + 2.0 * gelu_c
        t2 = jnp.tanh(a2 * p2)
        s2 = 1.0 + t2
        h2 = (a2 * s2).astype(bf16)
        d2 = s2 * (1.0 + (1.0 - t2) * (a2 * (3.0 * p2 - 4.0 * gelu_c)))
        tau = dot(ow[...], h2)[0:8]
        tbase = s * (CX * TROW) + part * (XC * TROW)
        err = jnp.concatenate(
            [
                (
                    tau[:, x * CY : (x + 1) * CY]
                    - tg[pl.ds(pl.multiple_of(tbase + x * TROW, TROW), TROW), :]
                )
                * scale
                for x in range(XC)
            ],
            axis=1,
        )
        err = jnp.concatenate([err, jnp.zeros((8, NC), f32)], axis=0).astype(bf16)
        g2 = (dot(wbo[...], err) * d2).astype(bf16)
        g1 = (dot(wb2[...], g2) * d1).astype(bf16)
        grad[176:184, :] += dot_nt(err, h2)[0:8]
        mix = dot_nt(h1x, g2)
        grad[0:128, :] += mix[0:128]
        grad[184:192, :] += mix[136:144]
        grad[128:176, :] += dot_nt(pats, g1)
        return 0

    lax.fori_loop(0, S * CX // XC, train, 0)

    seg = GROWS // n_sy
    for j in range(n_sy):
        gseg[j] = grad[j * seg : (j + 1) * seg, :]

    def a_copy(k):
        to = lax.rem(isy + k, n_sy)
        return pltpu.make_async_remote_copy(
            src_ref=gseg.at[to], dst_ref=ra.at[isy],
            send_sem=a_s.at[to], recv_sem=a_r.at[isy],
            device_id=(isx, to, igr), device_id_type=MESH,
        )

    def a_arrival(k):
        of = lax.rem(isy + k, n_sy)
        return pltpu.make_async_remote_copy(
            src_ref=gseg.at[of], dst_ref=ra.at[of],
            send_sem=a_s.at[of], recv_sem=a_r.at[of],
            device_id=(isx, of, igr), device_id_type=MESH,
        )

    def b_copy(k, mine):
        at = lax.rem(ib + k, n_b)
        of = ib if mine else at
        return pltpu.make_async_remote_copy(
            src_ref=sb_sum, dst_ref=rb.at[of],
            send_sem=b_s.at[at], recv_sem=b_r.at[of],
            device_id=(at // n_grp, isy, lax.rem(at, n_grp)), device_id_type=MESH,
        )

    def c_copy(k, mine):
        at = lax.rem(isy + k, n_sy)
        of = isy if mine else at
        return pltpu.make_async_remote_copy(
            src_ref=fin, dst_ref=rc.at[of],
            send_sem=c_s.at[at], recv_sem=c_r.at[of],
            device_id=(isx, at, igr), device_id_type=MESH,
        )

    def each(count, act):
        def step(k, _):
            act(k)
            return 0

        lax.fori_loop(1, count, step, 0)

    ra[isy] = gseg[isy]
    each(n_sy, lambda k: a_copy(k).start())

    def second():
        each(n_sy, lambda k: a_arrival(k).wait_recv())
        total = ra[0]
        for j in range(1, n_sy):
            total = total + ra[j]
        sb_sum[...] = total
        rb[ib] = total
        each(n_b, lambda k: b_copy(k, True).start())

    def third():
        each(n_b, lambda k: b_copy(k, False).wait_recv())
        total = rb[0]
        for j in range(1, n_b):
            total = total + rb[j]
        fin[...] = total
        rc[isy] = total
        each(n_sy, lambda k: c_copy(k, True).start())

    qf[...] = jnp.ones(qf.shape, f32)
    for copy in halo[0:8]:
        copy.wait_recv()
    lane24 = lanes((24, CY))
    for side in (0, 1):
        left, mid, right = rowdst[side, 0], rowdst[side, 1], rowdst[side, 2]
        shifted = (
            jnp.where(lane24 == 0, pltpu.roll(left, 1, 1), pltpu.roll(mid, 1, 1)),
            mid,
            jnp.where(
                lane24 == CY - 1, pltpu.roll(right, CY - 1, 1), pltpu.roll(mid, CY - 1, 1)
            ),
        )
        at = side * (CX + 1) * BLK
        for b in range(3):
            hr[...] = shifted[b]
            for c in range(3):
                qf[pl.ds(at + c * 3 + b, PZ, stride=PLANE), :] = hr[8 * c : 8 * c + 8, :]
    cc[...] = jnp.where(
        lax.rem(lane, 2) == 0, pltpu.roll(coldst[1], CY - 1, 1), pltpu.roll(coldst[0], 1, 1)
    )

    def build(p, _):
        for c in range(3):
            j = c * PZ + p
            v = vel[pl.ds(pl.multiple_of(j * CX, CX), CX), :]
            edge = pltpu.roll(cc[...], CY - 1 - 2 * j, 1)
            at = p * PLANE + BLK + c * 3
            qf[pl.ds(at, CX, stride=BLK), :] = jnp.where(lane == 0, edge, pltpu.roll(v, 1, 1))
            qf[pl.ds(at + 1, CX, stride=BLK), :] = v
            qf[pl.ds(at + 2, CX, stride=BLK), :] = jnp.where(
                lane == CY - 1, edge, pltpu.roll(v, CY - 1, 1)
            )
        base = pl.ds(pl.multiple_of(p * PLANE, BLK), PLANE)
        qb[base, :] = qf[base, :].astype(bf16)
        return 0

    lax.fori_loop(0, PZ, build, 0)

    per = CX // XC
    chunks = PZ * per

    def where_is(i):
        turn = i // per
        p = jnp.where(turn == 0, 0, jnp.where(turn == 1, PZ - 1, turn - 1))
        return p, lax.rem(i, per)

    def patches_of(i):
        p, part = where_is(i)
        return load_patches(qb, p * PLANE + part * (XC * BLK), XC)

    def stage_conv(i):
        pats = patches_of(i)
        q1[...] = gate(dot(cw[:, 0:96], jnp.concatenate([pats, pats], axis=0)))

    def stage_mix(i):
        pats = patches_of(i)
        m2 = dot(mw[:, 0:224], jnp.concatenate([q1[...], pats, pats], axis=0))
        q2[...] = gate(m2[0:128])
        lin[...] = m2[128:136] + m2[136:144]

    def stage_out(i):
        p, part = where_is(i)
        tau = dot(ow[...], q2[...])[0:8] + lin[...]
        at = (p + 1) * TPLANE + (part * XC + 1) * TROW
        for x in range(XC):
            stress[pl.ds(pl.multiple_of(at + x * TROW, TROW), TROW), :] = tau[
                :, x * CY : (x + 1) * CY
            ]

    def z_copies():
        out = []
        for side, p in ((0, PZ), (1, 1)):
            out.append(
                pltpu.make_async_remote_copy(
                    src_ref=stress.at[pl.ds(p * TPLANE + TROW, CX * TROW)],
                    dst_ref=stress.at[pl.ds((PZ + 1) * side * TPLANE + TROW, CX * TROW)],
                    send_sem=ss.at[side],
                    recv_sem=srv.at[side],
                    device_id=(isx, isy, other),
                    device_id_type=MESH,
                )
            )
        return out

    zs = z_copies()

    def infer(i, _):
        stage_out(jnp.clip(i - 2, 0, chunks - 1))
        stage_mix(jnp.clip(i - 1, 0, chunks - 1))
        stage_conv(jnp.minimum(i, chunks - 1))

        @pl.when(i == 2 * per + 1)
        def _():
            for copy in zs:
                copy.start()

        @pl.when(i == 8)
        def _():
            second()

        @pl.when(i == 13)
        def _():
            third()

        return 0

    q1[...] = jnp.zeros(q1.shape, bf16)
    q2[...] = jnp.zeros(q2.shape, bf16)
    lin[...] = jnp.zeros(lin.shape, f32)
    lax.fori_loop(0, chunks + 2, infer, 0)

    for c in range(3):
        for side, x in ((0, 1), (1, CX)):
            srowsrc[side, 8 * c : 8 * c + 8, :] = stress[
                pl.ds(TPLANE + x * TROW + DX[c], PZ, stride=TPLANE), :
            ]

    def pack_stress(p, acc):
        for c in range(3):
            j = c * PZ + p
            v = stress[pl.ds((p + 1) * TPLANE + TROW + DY[c], CX, stride=TROW), :]
            acc = jnp.where(lane // 2 == j, pltpu.roll(v, 2 * j + 1, 1), acc)
        return acc

    scolsrc[...] = lax.fori_loop(0, PZ, pack_stress, jnp.zeros((CX, CY), f32))
    edges = []
    for side, to_x in ((0, up_x), (1, down_x)):
        edges.append(
            pltpu.make_async_remote_copy(
                src_ref=srowsrc.at[1 - side],
                dst_ref=srowdst.at[side],
                send_sem=ss.at[2 + side],
                recv_sem=srv.at[2 + side],
                device_id=(to_x, isy, igr),
                device_id_type=MESH,
            )
        )
    for side, to_y in ((0, ys[2]), (1, ys[0])):
        edges.append(
            pltpu.make_async_remote_copy(
                src_ref=scolsrc,
                dst_ref=scoldst.at[side],
                send_sem=ss.at[4 + side],
                recv_sem=srv.at[4 + side],
                device_id=(isx, to_y, igr),
                device_id_type=MESH,
            )
        )
    for copy in edges:
        copy.start()

    for copy in halo[8:10]:
        copy.wait_recv()

    def viscous(p, below, above):
        for c in range(3):
            at = p * PLANE + BLK + c * 3

            def pick_at(start):
                return qf[pl.ds(start, CX, stride=BLK), :]

            mid = pick_at(at + 1)
            total = pick_at(at) + pick_at(at + 2)
            total = total + pick_at(at + 1 - BLK) + pick_at(at + 1 + BLK)
            total = total + below(c) + above(c) - 6.0 * mid
            tend[pl.ds(pl.multiple_of((c * PZ + p) * CX, CX), CX), :] = visc * total

    def plane_of(p):
        return lambda c: vel[pl.ds(pl.multiple_of((c * PZ + p) * CX, CX), CX), :]

    def ghost(side):
        return lambda c: zdst[side, c * CX : (c + 1) * CX, :]

    viscous(0, ghost(0), plane_of(1))

    def inner(p, _):
        viscous(p, plane_of(p - 1), plane_of(p + 1))
        return 0

    lax.fori_loop(1, PZ - 1, inner, 0)
    viscous(PZ - 1, plane_of(PZ - 2), ghost(1))

    each(n_sy, lambda k: c_copy(k, False).wait_recv())
    for j in range(n_sy):
        grad[j * seg : (j + 1) * seg, :] = rc[j]
    gmix[...] = grad[0:128, :]
    for c in range(3):
        for a in range(3):
            at = 128 + a * BLK + c * 3
            gconv[c * 9 + 3 * a : c * 9 + 3 * a + 3, :] = grad[at : at + 3, :]
    gbconv[...] = grad[137:138, :]
    gbmix[...] = grad[185:186, :]
    gout[...] = jnp.concatenate(
        [grad[176:184, :], jnp.zeros((120, 128), f32)], axis=0
    ).T[:, 0:6]

    for copy in zs:
        copy.wait_send()
    for copy in edges + zs:
        copy.wait_recv()
    for side in (0, 1):
        for c in range(3):
            stress[
                pl.ds(TPLANE + side * (CX + 1) * TROW + DX[c], PZ, stride=TPLANE), :
            ] = srowdst[side, 8 * c : 8 * c + 8, :]
    scc[...] = jnp.where(
        lax.rem(lane, 2) == 0, pltpu.roll(scoldst[1], CY - 1, 1), pltpu.roll(scoldst[0], 1, 1)
    )
    half = 0.25 / lam

    def diverge(p, _):
        for c in range(3):
            j = c * PZ + p

            def pick_at(plane, x, comp):
                return stress[pl.ds((p + plane) * TPLANE + x * TROW + comp, CX, stride=TROW), :]

            along_x = pick_at(1, 2, DX[c]) - pick_at(1, 0, DX[c])
            v = pick_at(1, 1, DY[c])
            edge = pltpu.roll(scc[...], CY - 1 - 2 * j, 1)
            along_y = jnp.where(lane == CY - 1, edge, pltpu.roll(v, CY - 1, 1)) - jnp.where(
                lane == 0, edge, pltpu.roll(v, 1, 1)
            )
            along_z = pick_at(2, 1, DZ[c]) - pick_at(0, 1, DZ[c])
            at = pl.ds(pl.multiple_of(j * CX, CX), CX)
            tend[at, :] = tend[at, :] - half * (along_x + along_y + along_z)
        return 0

    lax.fori_loop(0, PZ, diverge, 0)

    for copy in halo + edges:
        copy.wait_send()
    each(n_sy, lambda k: a_copy(k).wait_send())
    each(n_b, lambda k: b_copy(k, True).wait_send())
    each(n_sy, lambda k: c_copy(k, True).wait_send())


def shards(velocity, target_stress, w_conv, b_conv, w_mix, b_mix, w_out, plane_offsets, trainer_map):
    n_sx, n_sy, n_grp = (lax.axis_size(a) for a in ("sx", "sy", "grp"))
    n_b = n_sx * n_grp
    seg = GROWS // n_sy
    gscale = 1.0 / math.sqrt(S * n_sx * n_sy * n_grp * CX * CY)
    vmem = pl.BlockSpec(memory_space=pltpu.VMEM)
    smem = pl.BlockSpec(memory_space=pltpu.SMEM)

    def buf(*shape, dtype=f32):
        return pltpu.VMEM(shape, dtype)

    def sems(count):
        return pltpu.SemaphoreType.DMA((count,))

    outs = pl.pallas_call(
        functools.partial(kernel, n_sx, n_sy, n_grp, gscale),
        out_shape=[
            jax.ShapeDtypeStruct((3 * PZ * CX, CY), f32),
            jax.ShapeDtypeStruct((27, 128), f32),
            jax.ShapeDtypeStruct((1, 128), f32),
            jax.ShapeDtypeStruct((128, 128), f32),
            jax.ShapeDtypeStruct((1, 128), f32),
            jax.ShapeDtypeStruct((128, 6), f32),
        ],
        in_specs=[vmem] * 7 + [smem, vmem],
        out_specs=[vmem] * 6,
        scratch_shapes=[
            buf(PZ * PLANE, CY), buf(PZ * PLANE, CY, dtype=bf16),
            buf(S * PLANE, CY), buf(S * PLANE, CY, dtype=bf16),
            buf(S * CX * TROW, CY),
            buf((PZ + 2) * TPLANE, CY),
            buf(128, 128, dtype=bf16), buf(144, 256, dtype=bf16), buf(16, 128, dtype=bf16),
            buf(128, 128, dtype=bf16), buf(128, 256, dtype=bf16),
            buf(128, 128, dtype=bf16), buf(128, 16, dtype=bf16),
            buf(128, 128), buf(256, 128),
            buf(128, NC, dtype=bf16), buf(128, NC, dtype=bf16), buf(8, NC),
            buf(GROWS, 128),
            buf(2, 24, CY), buf(2, 3, 24, CY), buf(CX, CY), buf(2, CX, CY),
            buf(2, 3 * CX, CY), buf(2, 3 * CX, CY),
            buf(24, CY), buf(CX, CY),
            buf(2, 24, CY), buf(2, 24, CY), buf(CX, CY), buf(2, CX, CY), buf(CX, CY),
            buf(n_sy, seg, 128), buf(n_sy, seg, 128),
            buf(seg, 128), buf(n_b, seg, 128),
            buf(seg, 128), buf(n_sy, seg, 128),
            sems(10), sems(10), sems(6), sems(6),
            sems(n_sy), sems(n_sy), sems(n_b), sems(n_b), sems(n_sy), sems(n_sy),
        ],
        compiler_params=pltpu.CompilerParams(
            collective_id=0, has_side_effects=True, vmem_limit_bytes=40 * 2**20
        ),
    )(
        velocity.reshape(3 * PZ * CX, CY),
        target_stress.reshape(6 * PZ * CX, CY),
        w_conv,
        b_conv.reshape(1, 128),
        w_mix,
        b_mix.reshape(1, 128),
        w_out,
        plane_offsets.reshape(S),
        trainer_map.reshape(1, n_sy * S),
    )
    return (
        outs[0].reshape(3, PZ, CX, CY),
        outs[1],
        outs[2].reshape(128),
        outs[3],
        outs[4].reshape(128),
        outs[5],
    )


def solution(mesh):
    in_specs = (
        P(None, "grp", "sx", "sy"),
        P(None, "grp", "sx", "sy"),
        P(),
        P(),
        P(),
        P(),
        P(),
        P("grp", "sx", "sy", None),
        P("grp", "sx", None, None),
    )
    out_specs = (P(None, "grp", "sx", "sy"), P(), P(), P(), P(), P())
    return jax.shard_map(shards, mesh=mesh, in_specs=in_specs, out_specs=out_specs, check_vma=False)
```

time: 277 us -> 51 us (0.18)
  blocking collectives: 80.8 us -> 0 us
  waiting for transfers between devices: 58.4 us -> 0 us
  local copies, waits for them, and re-layouts: 57.7 us -> 6.66 us
  Pallas kernels: 0 us -> 43.4 us
  matrix products: 33.7 us -> 0 us
  starting transfers between devices: 18.3 us -> 0 us
  between operations: 14.4 us -> 0.74 us
  other arithmetic: 12 us -> 0 us
    psum x1 -> x0, blocking collectives: 80.8 us -> none  [shards(): lax.psum((grads[0], grads[1], grads[2], grads[3], grads[4]), ('sx', 'sy',...]
    psum x1 -> x0, waiting for transfers between devices: 52.2 us -> none  [shards(): lax.psum((grads[0], grads[1], grads[2], grads[3], grads[4]), ('sx', 'sy',...]
    pallas_call x0 -> x1, Pallas kernels: none -> 43.4 us  [shards(): pl.pallas_call(functools.partial(kernel, n_sx, n_sy, n_grp, gscale), out_...]
    dot_general x24 -> x0, matrix products: 33.7 us -> none  [the longest x9 15.1 us: forward(): jnp.dot(hidden_one, w_mix, preferred_element_type=jnp.float32) + b_mix]
    dynamic_update_slice x8 -> x0, local copies, waits for them, and re-layouts: 30.6 us -> none  [closure(): lax.map(infer, jnp.transpose(field_b, (1, 0, 2, 3)))]
    ppermute x12 -> x0, starting transfers between devices: 18.3 us -> none  [the longest x6 9.26 us: with_halo(): lax.ppermute(tail, axis, [(i, (i + 1) % count) for i in range(count)])]
    squeeze x9 -> x0, local copies, waits for them, and re-layouts: 6.78 us -> none  [the longest x8 6.67 us: closure(): lax.map(infer, jnp.transpose(field_b, (1, 0, 2, 3)))]
    ppermute x12 -> x0, waiting for transfers between devices: 6.16 us -> none  [the longest x6 4.66 us: with_halo(): lax.ppermute(tail, axis, [(i, (i + 1) % count) for i in range(count)])]
  transfers between devices with their start and end apart: 13 -> 0, of which waited for: 4 -> 0; matrix products, arithmetic and copies ran while one was open for 31% -> 0% of each run, Pallas kernels for 0% -> 0%
where the time goes in v1:
time: 51 us; the launch traced here: 50.8 us
  Pallas kernels  43.4 us (85%)
  local copies, waits for them, and re-layouts  6.66 us (13%)
  between operations  0.74 us (1%)
    pallas_call x1, Pallas kernels, shards(): pl.pallas_call(functools.partial(kernel, n_sx, n_sy, n_grp, gscale), out_...  43.4 us
    unnamed x23, local copies, waits for them, and re-layouts  6.66 us

profile of v1, /device:TPU:1, one launch (start us, length us, event | category | flops | bytes accessed | tf_op | source)
XLA Modules:
  0.0 50.8 jit_solution(9659255085680105207)
XLA Ops:
  0.6 0.0 copy-start.2
  0.6 0.0 copy-start.3
  0.7 0.0 copy-start.4
  0.7 0.0 copy-start.5
  0.7 0.0 copy-start.6
  0.7 0.0 copy-start.7
  0.7 0.8 %copy.15.wo = bf16[128,6]{1,0:T(8,128)(2,1)S(1)} copy(bf16[128,6]{0,1:T(8,128)(2,1)} %param.15) | data formatting | bytes 3072 | tf_op args[6]
  1.5 0.0 copy-done.2
  1.5 0.0 copy-done.3
  1.6 0.0 copy-done.4
  1.6 0.0 copy-done.5
  1.6 0.0 copy-done.6
  1.6 0.0 copy-done.7
  1.6 0.0 copy-start
  1.6 1.1 %copy-done = f32[6,8,32,128]{3,2,1,0:T(8,128)S(1)} copy-done((f32[6,8,32,128]{3,2,1,0:T(8,128)S(1)}, f32[6,8,32,128]{3,2,1,0:T(8,128)}, u32[]{:S(2)}) %copy-start) | copy-done | bytes 786456
  2.7 0.0 copy-start.1
  2.7 1.0 %copy-done.1 = f32[3,8,32,128]{3,2,1,0:T(8,128)S(1)} copy-done((f32[3,8,32,128]{3,2,1,0:T(8,128)S(1)}, f32[3,8,32,128]{3,2,1,0:T(8,128)}, u32[]{:S(2)}) %copy-start.1) | copy-done | bytes 393240
  3.7 43.4 %shard_map.136 = (f32[768,128]{1,0:T(8,128)S(1)}, f32[27,128]{1,0:T(8,128)S(1)}, f32[1,128]{1,0:T(1,128)S(1)}, f32[128,128]{1,0:T(8,128)S(1)}, f32[1,128]{1,0:T(1,128)S(1)}, /*index=5*/f32[128,6]{1,0:T(8,128)S(1)}) custom-call(f32[768,128]{1,0:T(8,128)S(1)} %bitcast.10, f32[1536,128]{1,0:T(8,128)S(1)} %bitcast.9, bf16[27,128]{1,0:T(8,128)(2,1)S(1)} %copy-done.3, ...), custom_call_target="tpu_custom_call" | custom-call | tf_op jit(solution)/shard_map/pallas_call | solution.py:622
  47.1 0.7 %copy.16 = f32[128,6]{0,1:T(8,128)} copy(f32[128,6]{1,0:T(8,128)S(1)} %get-tuple-element.23) | data formatting | bytes 6144
  47.8 0.7 %copy.22 = f32[3,8,32,128]{3,2,1,0:T(8,128)} copy(f32[3,8,32,128]{3,2,1,0:T(8,128)S(1)} %bitcast.11) | data formatting | bytes 786432
  48.5 0.6 %copy.23 = f32[27,128]{1,0:T(8,128)} copy(f32[27,128]{1,0:T(8,128)S(1)} %get-tuple-element.31) | data formatting | bytes 27648
  49.2 0.5 %copy.24 = f32[128]{0:T(128)} copy(f32[128]{0:T(128)S(1)} %bitcast.17) | data formatting | bytes 1024
  49.7 0.6 %copy.25 = f32[128,128]{1,0:T(8,128)} copy(f32[128,128]{1,0:T(8,128)S(1)} %get-tuple-element.33) | data formatting | bytes 131072
  50.3 0.5 %copy.26 = f32[128]{0:T(128)} copy(f32[128]{0:T(128)S(1)} %bitcast.16) | data formatting | bytes 1024
Async XLA Ops:
  0.6 0.9 %copy-start.2 = (bf16[128,128]{1,0:T(8,128)(2,1)S(1)}, bf16[128,128]{1,0:T(8,128)(2,1)}, u32[]{:S(2)}) copy-start(bf16[128,128]{1,0:T(8,128)(2,1)} %wm.1) | copy-start | bytes 98308
  0.6 0.9 %copy-start.3 = (bf16[27,128]{1,0:T(8,128)(2,1)S(1)}, bf16[27,128]{1,0:T(8,128)(2,1)}, u32[]{:S(2)}) copy-start(bf16[27,128]{1,0:T(8,128)(2,1)} %wc.1) | copy-start | bytes 20740
  0.7 0.9 %copy-start.4 = (f32[128]{0:T(128)S(1)}, f32[128]{0:T(128)}, u32[]{:S(2)}) copy-start(f32[128]{0:T(128)} %param.12) | copy-start | bytes 1540
  0.7 0.9 %copy-start.5 = (f32[128]{0:T(128)S(1)}, f32[128]{0:T(128)}, u32[]{:S(2)}) copy-start(f32[128]{0:T(128)} %param.14) | copy-start | bytes 1540
  0.7 0.9 %copy-start.6 = (s32[1,1,1,2]{3,2,1,0:T(1,128)S(1)}, s32[1,1,1,2]{3,2,1,0:T(1,128)}, u32[]{:S(2)}) copy-start(s32[1,1,1,2]{3,2,1,0:T(1,128)} %param.16) | copy-start | bytes 28
  0.7 0.9 %copy-start.7 = (s32[1,1,32,1]{2,3,1,0:T(1,128)S(1)}, s32[1,1,32,1]{2,3,1,0:T(1,128)}, u32[]{:S(2)}) copy-start(s32[1,1,32,1]{2,3,1,0:T(1,128)} %param.17) | copy-start | bytes 388
  1.6 1.1 %copy-start = (f32[6,8,32,128]{3,2,1,0:T(8,128)S(1)}, f32[6,8,32,128]{3,2,1,0:T(8,128)}, u32[]{:S(2)}) copy-start(f32[6,8,32,128]{3,2,1,0:T(8,128)} %param.10) | copy-start | bytes 2359300
  2.7 1.0 %copy-start.1 = (f32[3,8,32,128]{3,2,1,0:T(8,128)S(1)}, f32[3,8,32,128]{3,2,1,0:T(8,128)}, u32[]{:S(2)}) copy-start(f32[3,8,32,128]{3,2,1,0:T(8,128)} %param.9) | copy-start | bytes 1179652

commit v2 on v1

--- a/solution.py
+++ b/solution.py
@@ -29,6 +29,9 @@
 TPLANE = (CX + 2) * TROW
 XC = 16
 NC = XC * CY
+PER = CX // XC
+ORDER = (0, 7, 1, 2, 3, 4, 5, 6)
+EARLY = 6
 GROWS = 192
 
 DX = (0, 3, 4)
@@ -53,6 +56,15 @@
 
 def gate(m):
     return (m * jnp.tanh(m * (m * m + shift_c))).astype(bf16)
+
+
+def gate_and_slope(m):
+    m = m.astype(bf16)
+    z = m * (m * m + bf16(shift_c))
+    t = jnp.tanh(z)
+    up = bf16(1.0) + t
+    down = bf16(1.0) - t
+    return m * up, up * (bf16(1.0) + down * (bf16(3.0) * z - bf16(2.0 * shift_c) * m))
 
 
 def lanes(shape):
@@ -75,14 +87,15 @@
 
 def kernel(
     n_sx, n_sy, n_grp, gscale,
-    vel, tgt, wc, bc, wm, bm, wo, offs, tmap,
+    vel_in, tgt_in, wc, bc, wm, bm, wo, offs, tmap,
     tend, gconv, gbconv, gmix, gbmix, gout,
-    qf, qb, sf, sb, tg, stress, cw, mw, ow, tw1, tw2, wb2, wbo, prep, prep2,
-    q1, q2, lin, grad,
+    vel, tgt,
+    qf, qb, sf, sb, tg, stress, cw, mw, ow, tw2, wb2, wbo, prep, prep2,
+    q1, q2, lin, grad, h1, d1, h2, d2, g2,
     rowsrc, rowdst, colsrc, coldst, zsrc, zdst, hr, cc,
     srowsrc, srowdst, scolsrc, scoldst, scc,
     gseg, ra, sb_sum, rb, fin, rc,
-    hs, hrv, ss, srv, a_s, a_r, b_s, b_r, c_s, c_r,
+    ins, hs, hrv, ss, srv, a_s, a_r, b_s, b_r, c_s, c_r,
 ):
     isx, isy, igr = lax.axis_index("sx"), lax.axis_index("sy"), lax.axis_index("grp")
     up_x, down_x = lax.rem(isx + 1, n_sx), lax.rem(isx + n_sx - 1, n_sx)
@@ -91,6 +104,13 @@
     n_b = n_sx * n_grp
     ib = isx * n_grp + igr
 
+    loads = [
+        pltpu.make_async_copy(vel_in, vel, ins.at[0]),
+        pltpu.make_async_copy(tgt_in, tgt, ins.at[1]),
+    ]
+    for copy in loads:
+        copy.start()
+
     barrier = pltpu.get_barrier_semaphore()
 
     def greet(device):
@@ -111,6 +131,48 @@
         for to_y in (ys[0], ys[2]):
             greet((to_x, to_y, igr))
 
+    prep[...] = jnp.zeros(prep.shape, f32)
+    for c in range(3):
+        for a in range(3):
+            prep[a * BLK + c * 3 : a * BLK + c * 3 + 3, :] = wc[
+                c * 9 + 3 * a : c * 9 + 3 * a + 3, :
+            ].astype(f32)
+    prep[9:10, :] = bc[...]
+    w1 = prep[...][0:48, :]
+    w2h = wm[...].astype(f32) * 0.5
+    row48 = rows((48, 128))
+    high, low = split(w1 * lam)
+    pad = jnp.zeros((32, 128), f32)
+    cw[...] = jnp.concatenate([high, low, pad], axis=0).T.astype(bf16)
+    comp = dot(w1 * lam, w2h, HIGH)
+    comp = comp + jnp.where(row48 == 9, lam * bm[...], 0.0)
+    comp_high, comp_low = split(comp)
+    pick = (lanes((16, 6)) == rows((16, 6))) | (lanes((16, 6)) + 8 == rows((16, 6)))
+    wo_rows = dot(pick.astype(bf16), wo[...])
+    ow[...] = jnp.where(rows((16, 128)) < 8, wo_rows, 0.0).astype(bf16)
+    prep[...] = jnp.zeros(prep.shape, f32)
+    prep[0:16, :] = wo_rows
+    wo16 = prep[...].T[:, 0:16]
+    outl = dot(jnp.concatenate([w2h, comp], axis=0), wo16, HIGH)
+    out_high, out_low = split(outl)
+    outl = jnp.where(lanes((176, 16)) < 8, out_high, out_low)
+    mw[0:128, 0:128] = w2h.T.astype(bf16)
+    tail = jnp.concatenate([comp_high, comp_low, pad], axis=0)
+    mw[0:128, 128:256] = tail.T.astype(bf16)
+    prep2[...] = jnp.zeros(prep2.shape, f32)
+    prep2[0:176, 0:16] = outl
+    mw[128:144, 0:128] = prep2[0:128, :].T[0:16, :].astype(bf16)
+    mw[128:144, 128:256] = prep2[128:256, :].T[0:16, :].astype(bf16)
+    bh, rest = split(lam * bm[...])
+    bmid, rest = split(rest)
+    row128 = rows((128, 128))
+    t2 = jnp.where(row128 == 9, bh, jnp.where(row128 == 10, bmid, jnp.where(row128 == 11, rest, 0.0)))
+    tw2[:, 0:128] = w2h.T.astype(bf16)
+    tw2[:, 128:256] = t2.T.astype(bf16)
+    wb2[...] = w2h.astype(bf16)
+    wbo[...] = (0.5 * jnp.where(lanes((128, 16)) < 8, wo16, 0.0)).astype(bf16)
+
+    loads[0].wait()
     for c in range(3):
         for side, x in ((0, 0), (1, CX - 1)):
             rowsrc[side, 8 * c : 8 * c + 8, :] = vel[pl.ds(c * PZ * CX + x, PZ, stride=CX), :]
@@ -126,8 +188,6 @@
         return acc
 
     colsrc[...] = lax.fori_loop(0, PZ, pack_cols, jnp.zeros((CX, CY), f32))
-
-    pl.semaphore_wait(barrier, (n_sy - 1) + (n_b - 1) + 4)
 
     def halo_copies():
         out = []
@@ -169,55 +229,22 @@
         return out
 
     halo = halo_copies()
-    for copy in halo:
-        copy.start()
-
-    prep[...] = jnp.zeros(prep.shape, f32)
-    for c in range(3):
-        for a in range(3):
-            prep[a * BLK + c * 3 : a * BLK + c * 3 + 3, :] = wc[
-                c * 9 + 3 * a : c * 9 + 3 * a + 3, :
-            ].astype(f32)
-    prep[9:10, :] = bc[...]
-    w1 = prep[...][0:48, :]
-    w2h = wm[...].astype(f32) * 0.5
-    row48 = rows((48, 128))
-    high, low = split(w1 * lam)
-    pad = jnp.zeros((32, 128), f32)
-    cw[...] = jnp.concatenate([high, low, pad], axis=0).T.astype(bf16)
-    comp = dot(w1 * lam, w2h, HIGH)
-    comp = comp + jnp.where(row48 == 9, lam * bm[...], 0.0)
-    comp_high, comp_low = split(comp)
-    pick16 = (
-        (lanes((6, 16)) == rows((6, 16))) | (lanes((6, 16)) == rows((6, 16)) + 8)
-    ).astype(bf16)
-    wo16 = dot(wo[...], pick16)
-    outl = dot(jnp.concatenate([w2h, comp], axis=0), wo16, HIGH)
-    out_high, out_low = split(outl)
-    outl = jnp.where(lanes((176, 16)) < 8, out_high, out_low)
-    mw[0:128, 0:128] = w2h.T.astype(bf16)
-    tail = jnp.concatenate([comp_high, comp_low, pad], axis=0)
-    mw[0:128, 128:256] = tail.T.astype(bf16)
-    prep2[...] = jnp.zeros(prep2.shape, f32)
-    prep2[0:176, 0:16] = outl
-    mw[128:144, 0:128] = prep2[0:128, :].T[0:16, :].astype(bf16)
-    mw[128:144, 128:256] = prep2[128:256, :].T[0:16, :].astype(bf16)
-    pick = (lanes((16, 6)) == rows((16, 6))).astype(bf16)
-    ow[...] = dot_nt(pick, wo[...]).astype(bf16)
-    half_b1 = 0.5 * bc[...]
-    bh, rest = split(half_b1)
-    bmid, rest = split(rest)
-    t1 = jnp.where(row48 == 9, bh, jnp.where(row48 == 10, bmid, jnp.where(row48 == 11, rest, 0.5 * w1)))
-    tw1[...] = jnp.concatenate([t1, pad, pad, pad[0:16]], axis=0).T.astype(bf16)
-    half_b2 = 0.5 * bm[...]
-    bh, rest = split(half_b2)
-    bmid, rest = split(rest)
-    row128 = rows((128, 128))
-    t2 = jnp.where(row128 == 9, bh, jnp.where(row128 == 10, bmid, jnp.where(row128 == 11, rest, 0.0)))
-    tw2[:, 0:128] = w2h.T.astype(bf16)
-    tw2[:, 128:256] = t2.T.astype(bf16)
-    wb2[...] = w2h.astype(bf16)
-    wbo[...] = (0.5 * jnp.where(lanes((128, 16)) < 8, wo16, 0.0)).astype(bf16)
+
+    def enter():
+        pl.semaphore_wait(barrier, (n_sy - 1) + (n_b - 1) + 4)
+        for copy in halo:
+            copy.start()
+
+    loads[1].wait()
+    names = tmap[...]
+    place = lanes(names.shape)
+
+    def scale_of(s):
+        dest = jnp.sum(jnp.where(place == isy * S + s, names, 0), axis=1, keepdims=True)
+        count = jnp.sum((names == dest).astype(f32), axis=1, keepdims=True)
+        return 2.0 * gscale / count
+
+    scales = [scale_of(s) for s in range(S)]
 
     sf[...] = jnp.ones(sf.shape, f32)
     zero8 = jnp.zeros((8, 128), f32)
@@ -244,62 +271,58 @@
                     w = v
                 sf[pl.ds(s * PLANE + BLK + c * 3 + b, CX, stride=BLK), :] = w
         for c in range(6):
-            tg[pl.ds(s * CX * TROW + c, CX, stride=TROW), :] = plane(tgt, c)
+            tg[pl.ds(s * CX * TROW + c, CX, stride=TROW), :] = scales[s] * plane(tgt, c)
     sb[...] = sf[...].astype(bf16)
     grad[...] = jnp.zeros(grad.shape, f32)
 
-    names = tmap[...]
-    place = lanes(names.shape)
-
-    def scale_of(s):
-        dest = jnp.sum(jnp.where(place == isy * S + s, names, 0), axis=1, keepdims=True)
-        count = jnp.sum((names == dest).astype(f32), axis=1, keepdims=True)
-        return jnp.broadcast_to(2.0 * gscale / count, (8, 128))
-
-    scales = [scale_of(s) for s in range(S)]
-
-    def train(i, _):
-        s = i // (CX // XC)
-        part = lax.rem(i, CX // XC)
-        scale = jnp.where(s == 0, scales[0], scales[1])
-        pats = load_patches(sb, s * PLANE + part * (XC * BLK), XC)
-        a1 = dot(tw1[:, 0:48], pats)
-        p1 = (8.0 * gelu_c * gelu_k) * (a1 * a1) + 2.0 * gelu_c
-        t1 = jnp.tanh(a1 * p1)
-        s1 = 1.0 + t1
-        h1 = (a1 * s1).astype(bf16)
-        d1 = s1 * (1.0 + (1.0 - t1) * (a1 * (3.0 * p1 - 4.0 * gelu_c)))
-        h1x = jnp.concatenate([h1, pats[0:16]], axis=0)
-        a2 = dot(tw2[:, 0:144], h1x)
-        p2 = (8.0 * gelu_c * gelu_k) * (a2 * a2) + 2.0 * gelu_c
-        t2 = jnp.tanh(a2 * p2)
-        s2 = 1.0 + t2
-        h2 = (a2 * s2).astype(bf16)
-        d2 = s2 * (1.0 + (1.0 - t2) * (a2 * (3.0 * p2 - 4.0 * gelu_c)))
-        tau = dot(ow[...], h2)[0:8]
-        tbase = s * (CX * TROW) + part * (XC * TROW)
-        err = jnp.concatenate(
-            [
-                (
-                    tau[:, x * CY : (x + 1) * CY]
-                    - tg[pl.ds(pl.multiple_of(tbase + x * TROW, TROW), TROW), :]
-                )
-                * scale
-                for x in range(XC)
-            ],
-            axis=1,
+    def sample_patches(k):
+        s, part = k // PER, k % PER
+        return load_patches(sb, s * PLANE + part * (XC * BLK), XC)
+
+    def train_conv(k):
+        pats = sample_patches(k)
+        m = dot(cw[:, 0:96], jnp.concatenate([pats, pats], axis=0))
+        h1[k], d1[k] = gate_and_slope(m)
+
+    def train_mix(k):
+        pats = sample_patches(k)
+        h2[k], d2[k] = gate_and_slope(
+            dot(tw2[:, 0:144], jnp.concatenate([h1[k], pats[0:16]], axis=0))
         )
-        err = jnp.concatenate([err, jnp.zeros((8, NC), f32)], axis=0).astype(bf16)
-        g2 = (dot(wbo[...], err) * d2).astype(bf16)
-        g1 = (dot(wb2[...], g2) * d1).astype(bf16)
-        grad[176:184, :] += dot_nt(err, h2)[0:8]
-        mix = dot_nt(h1x, g2)
+
+    def train_out(k):
+        s, part = k // PER, k % PER
+        tau = dot(ow[...], h2[k])[0:8] * (scales[s] * (0.5 / lam))
+        at = s * (CX * TROW) + part * (XC * TROW)
+        target = jnp.concatenate(
+            [tg[at + x * TROW : at + (x + 1) * TROW, :] for x in range(XC)], axis=1
+        )
+        err = jnp.concatenate([tau - target, jnp.zeros((8, NC), f32)], axis=0).astype(bf16)
+        g2[k] = dot(wbo[...], err).astype(bf16) * d2[k]
+        grad[176:184, :] += dot_nt(err, h2[k])[0:8]
+
+    def train_back(k):
+        pats = sample_patches(k)
+        g1 = dot(wb2[...], g2[k]).astype(bf16) * d1[k]
+        mix = dot_nt(jnp.concatenate([h1[k], pats[0:16]], axis=0), g2[k])
         grad[0:128, :] += mix[0:128]
         grad[184:192, :] += mix[136:144]
         grad[128:176, :] += dot_nt(pats, g1)
-        return 0
-
-    lax.fori_loop(0, S * CX // XC, train, 0)
+
+    parts = S * PER
+    for k in range(parts + 3):
+        if 0 <= k - 3:
+            train_back(k - 3)
+        if 0 <= k - 2 < parts:
+            train_out(k - 2)
+        if 0 <= k - 1 < parts:
+            train_mix(k - 1)
+        if k < parts:
+            train_conv(k)
+        if k == 2:
+            enter()
+    grad[0:128, :] = grad[0:128, :] * (0.5 / lam)
+    grad[176:184, :] = grad[176:184, :] * (0.5 / lam)
 
     seg = GROWS // n_sy
     for j in range(n_sy):
@@ -389,7 +412,7 @@
         lax.rem(lane, 2) == 0, pltpu.roll(coldst[1], CY - 1, 1), pltpu.roll(coldst[0], 1, 1)
     )
 
-    def build(p, _):
+    def build(p):
         for c in range(3):
             j = c * PZ + p
             v = vel[pl.ds(pl.multiple_of(j * CX, CX), CX), :]
@@ -402,40 +425,25 @@
             )
         base = pl.ds(pl.multiple_of(p * PLANE, BLK), PLANE)
         qb[base, :] = qf[base, :].astype(bf16)
-        return 0
-
-    lax.fori_loop(0, PZ, build, 0)
-
-    per = CX // XC
-    chunks = PZ * per
-
-    def where_is(i):
-        turn = i // per
-        p = jnp.where(turn == 0, 0, jnp.where(turn == 1, PZ - 1, turn - 1))
-        return p, lax.rem(i, per)
-
-    def patches_of(i):
-        p, part = where_is(i)
-        return load_patches(qb, p * PLANE + part * (XC * BLK), XC)
-
-    def stage_conv(i):
-        pats = patches_of(i)
-        q1[...] = gate(dot(cw[:, 0:96], jnp.concatenate([pats, pats], axis=0)))
-
-    def stage_mix(i):
-        pats = patches_of(i)
-        m2 = dot(mw[:, 0:224], jnp.concatenate([q1[...], pats, pats], axis=0))
-        q2[...] = gate(m2[0:128])
-        lin[...] = m2[128:136] + m2[136:144]
-
-    def stage_out(i):
-        p, part = where_is(i)
-        tau = dot(ow[...], q2[...])[0:8] + lin[...]
-        at = (p + 1) * TPLANE + (part * XC + 1) * TROW
+
+    def patches_of(k):
+        return load_patches(qb, ORDER[k // PER] * PLANE + (k % PER) * (XC * BLK), XC)
+
+    def stage_conv(k):
+        pats = patches_of(k)
+        q1[k % 2] = gate(dot(cw[:, 0:96], jnp.concatenate([pats, pats], axis=0)))
+
+    def stage_mix(k):
+        pats = patches_of(k)
+        m2 = dot(mw[:, 0:224], jnp.concatenate([q1[k % 2], pats, pats], axis=0))
+        q2[k % 2] = gate(m2[0:128])
+        lin[k % 2] = m2[128:136] + m2[136:144]
+
+    def stage_out(k):
+        tau = dot(ow[...], q2[k % 2])[0:8] + lin[k % 2]
+        at = (ORDER[k // PER] + 1) * TPLANE + (k % PER * XC + 1) * TROW
         for x in range(XC):
-            stress[pl.ds(pl.multiple_of(at + x * TROW, TROW), TROW), :] = tau[
-                :, x * CY : (x + 1) * CY
-            ]
+            stress[at + x * TROW : at + (x + 1) * TROW, :] = tau[:, x * CY : (x + 1) * CY]
 
     def z_copies():
         out = []
@@ -454,70 +462,75 @@
 
     zs = z_copies()
 
-    def infer(i, _):
-        stage_out(jnp.clip(i - 2, 0, chunks - 1))
-        stage_mix(jnp.clip(i - 1, 0, chunks - 1))
-        stage_conv(jnp.minimum(i, chunks - 1))
-
-        @pl.when(i == 2 * per + 1)
-        def _():
+    scolsrc[...] = jnp.zeros(scolsrc.shape, f32)
+    srowsrc[...] = jnp.zeros(srowsrc.shape, f32)
+
+    def edge_copies(group):
+        out = []
+        for side, to_x in ((0, up_x), (1, down_x)):
+            out.append(
+                pltpu.make_async_remote_copy(
+                    src_ref=srowsrc.at[group, 1 - side],
+                    dst_ref=srowdst.at[group, side],
+                    send_sem=ss.at[2 + 4 * group + side],
+                    recv_sem=srv.at[2 + 4 * group + side],
+                    device_id=(to_x, isy, igr),
+                    device_id_type=MESH,
+                )
+            )
+        for side, to_y in ((0, ys[2]), (1, ys[0])):
+            out.append(
+                pltpu.make_async_remote_copy(
+                    src_ref=scolsrc.at[group],
+                    dst_ref=scoldst.at[group, side],
+                    send_sem=ss.at[4 + 4 * group + side],
+                    recv_sem=srv.at[4 + 4 * group + side],
+                    device_id=(isx, to_y, igr),
+                    device_id_type=MESH,
+                )
+            )
+        return out
+
+    edges = [edge_copies(0), edge_copies(1)]
+    groups = (ORDER[:EARLY], ORDER[EARLY:])
+
+    def send_edges(group):
+        acc = jnp.zeros((CX, CY), f32)
+        for p in groups[group]:
+            for c in range(3):
+                j = c * PZ + p
+                at = (p + 1) * TPLANE
+                for side, x in ((0, 1), (1, CX)):
+                    srowsrc[group, side, j : j + 1, :] = stress[
+                        at + x * TROW + DX[c] : at + x * TROW + DX[c] + 1, :
+                    ]
+                v = stress[pl.ds(at + TROW + DY[c], CX, stride=TROW), :]
+                acc = jnp.where(lane // 2 == j, pltpu.roll(v, 2 * j + 1, 1), acc)
+        scolsrc[group] = acc
+        for copy in edges[group]:
+            copy.start()
+
+    chunks = PZ * PER
+    build(ORDER[0])
+    for k in range(chunks + 2):
+        if k % PER == 0 and k // PER + 1 < PZ:
+            build(ORDER[k // PER + 1])
+        if 0 <= k - 2:
+            stage_out(k - 2)
+        if 0 <= k - 1 < chunks:
+            stage_mix(k - 1)
+        if k < chunks:
+            stage_conv(k)
+        if k - 2 == 2 * PER - 1:
             for copy in zs:
                 copy.start()
-
-        @pl.when(i == 8)
-        def _():
+        if k - 2 == EARLY * PER - 1:
+            send_edges(0)
+        if k == 8:
             second()
-
-        @pl.when(i == 13)
-        def _():
+        if k == 14:
             third()
-
-        return 0
-
-    q1[...] = jnp.zeros(q1.shape, bf16)
-    q2[...] = jnp.zeros(q2.shape, bf16)
-    lin[...] = jnp.zeros(lin.shape, f32)
-    lax.fori_loop(0, chunks + 2, infer, 0)
-
-    for c in range(3):
-        for side, x in ((0, 1), (1, CX)):
-            srowsrc[side, 8 * c : 8 * c + 8, :] = stress[
-                pl.ds(TPLANE + x * TROW + DX[c], PZ, stride=TPLANE), :
-            ]
-
-    def pack_stress(p, acc):
-        for c in range(3):
-            j = c * PZ + p
-            v = stress[pl.ds((p + 1) * TPLANE + TROW + DY[c], CX, stride=TROW), :]
-            acc = jnp.where(lane // 2 == j, pltpu.roll(v, 2 * j + 1, 1), acc)
-        return acc
-
-    scolsrc[...] = lax.fori_loop(0, PZ, pack_stress, jnp.zeros((CX, CY), f32))
-    edges = []
-    for side, to_x in ((0, up_x), (1, down_x)):
-        edges.append(
-            pltpu.make_async_remote_copy(
-                src_ref=srowsrc.at[1 - side],
-                dst_ref=srowdst.at[side],
-                send_sem=ss.at[2 + side],
-                recv_sem=srv.at[2 + side],
-                device_id=(to_x, isy, igr),
-                device_id_type=MESH,
-            )
-        )
-    for side, to_y in ((0, ys[2]), (1, ys[0])):
-        edges.append(
-            pltpu.make_async_remote_copy(
-                src_ref=scolsrc,
-                dst_ref=scoldst.at[side],
-                send_sem=ss.at[4 + side],
-                recv_sem=srv.at[4 + side],
-                device_id=(isx, to_y, igr),
-                device_id_type=MESH,
-            )
-        )
-    for copy in edges:
-        copy.start()
+    send_edges(1)
 
     for copy in halo[8:10]:
         copy.wait_recv()
@@ -560,25 +573,11 @@
             gconv[c * 9 + 3 * a : c * 9 + 3 * a + 3, :] = grad[at : at + 3, :]
     gbconv[...] = grad[137:138, :]
     gbmix[...] = grad[185:186, :]
-    gout[...] = jnp.concatenate(
-        [grad[176:184, :], jnp.zeros((120, 128), f32)], axis=0
-    ).T[:, 0:6]
-
-    for copy in zs:
-        copy.wait_send()
-    for copy in edges + zs:
-        copy.wait_recv()
-    for side in (0, 1):
-        for c in range(3):
-            stress[
-                pl.ds(TPLANE + side * (CX + 1) * TROW + DX[c], PZ, stride=TPLANE), :
-            ] = srowdst[side, 8 * c : 8 * c + 8, :]
-    scc[...] = jnp.where(
-        lax.rem(lane, 2) == 0, pltpu.roll(scoldst[1], CY - 1, 1), pltpu.roll(scoldst[0], 1, 1)
-    )
+    gout[...] = grad[176:182, :]
+
     half = 0.25 / lam
 
-    def diverge(p, _):
+    def diverge(p):
         for c in range(3):
             j = c * PZ + p
 
@@ -592,17 +591,38 @@
                 lane == 0, edge, pltpu.roll(v, 1, 1)
             )
             along_z = pick_at(2, 1, DZ[c]) - pick_at(0, 1, DZ[c])
-            at = pl.ds(pl.multiple_of(j * CX, CX), CX)
+            at = pl.ds(j * CX, CX)
             tend[at, :] = tend[at, :] - half * (along_x + along_y + along_z)
-        return 0
-
-    lax.fori_loop(0, PZ, diverge, 0)
-
-    for copy in halo + edges:
+
+    for copy in zs:
+        copy.wait_send()
+        copy.wait_recv()
+    for group in (0, 1):
+        for copy in edges[group]:
+            copy.wait_recv()
+        for p in groups[group]:
+            for side in (0, 1):
+                for c in range(3):
+                    at = (p + 1) * TPLANE + side * (CX + 1) * TROW + DX[c]
+                    stress[at : at + 1, :] = srowdst[group, side, c * PZ + p : c * PZ + p + 1, :]
+        scc[...] = jnp.where(
+            lax.rem(lane, 2) == 0,
+            pltpu.roll(scoldst[group, 1], CY - 1, 1),
+            pltpu.roll(scoldst[group, 0], 1, 1),
+        )
+        for p in groups[group]:
+            diverge(p)
+
+    for copy in halo + edges[0] + edges[1]:
         copy.wait_send()
     each(n_sy, lambda k: a_copy(k).wait_send())
     each(n_b, lambda k: b_copy(k, True).wait_send())
     each(n_sy, lambda k: c_copy(k, True).wait_send())
+
+
+def write_out(*refs):
+    for source, result in zip(refs[:6], refs[6:]):
+        result[...] = source[...]
 
 
 def shards(velocity, target_stress, w_conv, b_conv, w_mix, b_mix, w_out, plane_offsets, trainer_map):
@@ -612,6 +632,7 @@
     gscale = 1.0 / math.sqrt(S * n_sx * n_sy * n_grp * CX * CY)
     vmem = pl.BlockSpec(memory_space=pltpu.VMEM)
     smem = pl.BlockSpec(memory_space=pltpu.SMEM)
+    hbm = pl.BlockSpec(memory_space=pltpu.HBM)
 
     def buf(*shape, dtype=f32):
         return pltpu.VMEM(shape, dtype)
@@ -627,33 +648,35 @@
             jax.ShapeDtypeStruct((1, 128), f32),
             jax.ShapeDtypeStruct((128, 128), f32),
             jax.ShapeDtypeStruct((1, 128), f32),
-            jax.ShapeDtypeStruct((128, 6), f32),
+            jax.ShapeDtypeStruct((6, 128), f32),
         ],
-        in_specs=[vmem] * 7 + [smem, vmem],
+        in_specs=[hbm] * 2 + [vmem] * 5 + [smem, vmem],
         out_specs=[vmem] * 6,
         scratch_shapes=[
+            buf(3 * PZ * CX, CY), buf(6 * PZ * CX, CY),
             buf(PZ * PLANE, CY), buf(PZ * PLANE, CY, dtype=bf16),
             buf(S * PLANE, CY), buf(S * PLANE, CY, dtype=bf16),
             buf(S * CX * TROW, CY),
             buf((PZ + 2) * TPLANE, CY),
             buf(128, 128, dtype=bf16), buf(144, 256, dtype=bf16), buf(16, 128, dtype=bf16),
-            buf(128, 128, dtype=bf16), buf(128, 256, dtype=bf16),
+            buf(128, 256, dtype=bf16),
             buf(128, 128, dtype=bf16), buf(128, 16, dtype=bf16),
             buf(128, 128), buf(256, 128),
-            buf(128, NC, dtype=bf16), buf(128, NC, dtype=bf16), buf(8, NC),
+            buf(2, 128, NC, dtype=bf16), buf(2, 128, NC, dtype=bf16), buf(2, 8, NC),
             buf(GROWS, 128),
+            *[buf(S * PER, 128, NC, dtype=bf16) for _ in range(5)],
             buf(2, 24, CY), buf(2, 3, 24, CY), buf(CX, CY), buf(2, CX, CY),
             buf(2, 3 * CX, CY), buf(2, 3 * CX, CY),
             buf(24, CY), buf(CX, CY),
-            buf(2, 24, CY), buf(2, 24, CY), buf(CX, CY), buf(2, CX, CY), buf(CX, CY),
+            buf(2, 2, 24, CY), buf(2, 2, 24, CY), buf(2, CX, CY), buf(2, 2, CX, CY), buf(CX, CY),
             buf(n_sy, seg, 128), buf(n_sy, seg, 128),
             buf(seg, 128), buf(n_b, seg, 128),
             buf(seg, 128), buf(n_sy, seg, 128),
-            sems(10), sems(10), sems(6), sems(6),
+            sems(2), sems(10), sems(10), sems(10), sems(10),
             sems(n_sy), sems(n_sy), sems(n_b), sems(n_b), sems(n_sy), sems(n_sy),
         ],
         compiler_params=pltpu.CompilerParams(
-            collective_id=0, has_side_effects=True, vmem_limit_bytes=40 * 2**20
+            collective_id=0, has_side_effects=True, vmem_limit_bytes=62 * 2**20
         ),
     )(
         velocity.reshape(3 * PZ * CX, CY),
@@ -662,17 +685,23 @@
         b_conv.reshape(1, 128),
         w_mix,
         b_mix.reshape(1, 128),
-        w_out,
+        w_out.T,
         plane_offsets.reshape(S),
         trainer_map.reshape(1, n_sy * S),
     )
+    outs = pl.pallas_call(
+        write_out,
+        out_shape=[jax.ShapeDtypeStruct(o.shape, o.dtype) for o in outs],
+        in_specs=[vmem] * 6,
+        out_specs=[vmem] * 6,
+    )(*outs)
     return (
         outs[0].reshape(3, PZ, CX, CY),
         outs[1],
         outs[2].reshape(128),
         outs[3],
         outs[4].reshape(128),
-        outs[5],
+        outs[5].T,
     )
 
 

time: 51 us -> 39.3 us (0.77)
  local copies, waits for them, and re-layouts: 6.66 us -> 0 us
  Pallas kernels: 43.4 us -> 38.5 us
    pallas_call x1, Pallas kernels: 43.4 us -> 36.7 us  [shards(): pl.pallas_call(functools.partial(kernel, n_sx, n_sy, n_grp, gscale), out_...]
    unnamed x23 -> x0, local copies, waits for them, and re-layouts: 6.66 us -> none
    pallas_call x0 -> x1, Pallas kernels: none -> 1.85 us  [shards(): pl.pallas_call(write_out, out_shape=[jax.ShapeDtypeStruct(o.shape, o.dtyp...]
where the time goes in v2:
time: 39.3 us; the launch traced here: 39.2 us
  Pallas kernels  38.5 us (98%)
  between operations  0.64 us (2%)
    pallas_call x1, Pallas kernels, shards(): pl.pallas_call(functools.partial(kernel, n_sx, n_sy, n_grp, gscale), out_...  36.7 us
    pallas_call x1, Pallas kernels, shards(): pl.pallas_call(write_out, out_shape=[jax.ShapeDtypeStruct(o.shape, o.dtyp...  1.85 us

profile of v2, /device:TPU:1, one launch (start us, length us, event | category | flops | bytes accessed | tf_op | source)
XLA Modules:
  0.0 39.2 jit_solution(17284693868019952758)
XLA Ops:
  0.6 36.7 %shard_map.136 = (f32[768,128]{1,0:T(8,128)}, f32[27,128]{1,0:T(8,128)}, f32[1,128]{1,0:T(1,128)}, f32[128,128]{1,0:T(8,128)}, f32[1,128]{1,0:T(1,128)}, /*index=5*/f32[6,128]{1,0:T(8,128)}) custom-call(f32[768,128]{1,0:T(8,128)} %bitcast.12, f32[1536,128]{1,0:T(8,128)} %bitcast.11, bf16[27,128]{1,0:T(8,128)(2,1)} %wc.1, f32[1,128]{1,0:T(1,128)} %bitcast.14, ...), custom_call_target="tpu_custom_call" | custom-call | tf_op jit(solution)/shard_map/pallas_call | solution.py:643
  37.3 1.8 %shard_map.137 = (f32[768,128]{1,0:T(8,128)}, f32[27,128]{1,0:T(8,128)}, f32[1,128]{1,0:T(1,128)}, f32[128,128]{1,0:T(8,128)}, f32[1,128]{1,0:T(1,128)}, /*index=5*/f32[6,128]{1,0:T(8,128)}) custom-call(f32[768,128]{1,0:T(8,128)} %get-tuple-element.18.refs_0_, f32[27,128]{1,0:T(8,128)} %get-tuple-element.19.refs_1_, f32[1,128]{1,0:T(1,128)} %get-tuple-element.20.refs_2_, ...), custom_call_target="tpu_custom_call" | custom-call | tf_op jit(solution)/shard_map/pallas_call | solution.py:692

commit v3 on v2

--- a/solution.py
+++ b/solution.py
@@ -92,17 +92,37 @@
     vel, tgt,
     qf, qb, sf, sb, tg, stress, cw, mw, ow, tw2, wb2, wbo, prep, prep2,
     q1, q2, lin, grad, h1, d1, h2, d2, g2,
-    rowsrc, rowdst, colsrc, coldst, zsrc, zdst, hr, cc,
-    srowsrc, srowdst, scolsrc, scoldst, scc,
-    gseg, ra, sb_sum, rb, fin, rc,
-    ins, hs, hrv, ss, srv, a_s, a_r, b_s, b_r, c_s, c_r,
+    rowsrc, colsrc, hdst, zsrc, zdst, hr, cc,
+    srowsrc, scolsrc, edst, scc,
+    ra, part_a, rb, part_b, rc, part_c, rd,
+    ins, hs, hrv, ss, srv, rs, rr,
 ):
     isx, isy, igr = lax.axis_index("sx"), lax.axis_index("sy"), lax.axis_index("grp")
     up_x, down_x = lax.rem(isx + 1, n_sx), lax.rem(isx + n_sx - 1, n_sx)
     ys = (lax.rem(isy + n_sy - 1, n_sy), isy, lax.rem(isy + 1, n_sy))
     other = 1 - igr
-    n_b = n_sx * n_grp
-    ib = isx * n_grp + igr
+    n_low = min(4, n_sy)
+    n_far = n_sy // n_low * n_grp
+    low, high = lax.rem(isy, n_low), isy // n_low
+    far = high * n_grp + igr
+
+    def in_sx(k):
+        return lax.rem(isx + k, n_sx)
+
+    def in_low(k):
+        return lax.rem(low + k, n_low)
+
+    def in_far(k):
+        return lax.rem(far + k, n_far)
+
+    def at_sx(i):
+        return (i, isy, igr)
+
+    def at_low(i):
+        return (isx, high * n_low + i, igr)
+
+    def at_far(i):
+        return (isx, i // n_grp * n_low + low, lax.rem(i, n_grp))
 
     loads = [
         pltpu.make_async_copy(vel_in, vel, ins.at[0]),
@@ -116,20 +136,22 @@
     def greet(device):
         pl.semaphore_signal(barrier, inc=1, device_id=device, device_id_type=MESH)
 
-    def greet_sy(k, _):
-        greet((isx, lax.rem(isy + k, n_sy), igr))
-        return 0
-
-    def greet_b(k, _):
-        at = lax.rem(ib + k, n_b)
-        greet((at // n_grp, isy, lax.rem(at, n_grp)))
-        return 0
-
-    lax.fori_loop(1, n_sy, greet_sy, 0)
-    lax.fori_loop(1, n_b, greet_b, 0)
-    for to_x in (up_x, down_x):
-        for to_y in (ys[0], ys[2]):
-            greet((to_x, to_y, igr))
+    friends = [at_sx(in_sx(k)) for k in range(1, n_sx)]
+    friends += [at_low(in_low(k)) for k in range(1, n_low)]
+    friends += [at_far(in_far(k)) for k in range(1, n_far)]
+    friends += [(isx, ys[0], igr), (isx, ys[2], igr)]
+    friends += [(to_x, to_y, igr) for to_x in (up_x, down_x) for to_y in (ys[0], ys[2])]
+    for device in friends:
+        greet(device)
+
+    def remote(src, dst, send, recv, device):
+        return pltpu.make_async_remote_copy(
+            src_ref=src, dst_ref=dst, send_sem=send, recv_sem=recv,
+            device_id=device, device_id_type=MESH,
+        )
+
+    def all_of(buffer, send, recv):
+        return remote(buffer, buffer, send, recv, at_sx(in_sx(1)))
 
     prep[...] = jnp.zeros(prep.shape, f32)
     for c in range(3):
@@ -141,9 +163,9 @@
     w1 = prep[...][0:48, :]
     w2h = wm[...].astype(f32) * 0.5
     row48 = rows((48, 128))
-    high, low = split(w1 * lam)
+    conv_high, conv_low = split(w1 * lam)
     pad = jnp.zeros((32, 128), f32)
-    cw[...] = jnp.concatenate([high, low, pad], axis=0).T.astype(bf16)
+    cw[...] = jnp.concatenate([conv_high, conv_low, pad], axis=0).T.astype(bf16)
     comp = dot(w1 * lam, w2h, HIGH)
     comp = comp + jnp.where(row48 == 9, lam * bm[...], 0.0)
     comp_high, comp_low = split(comp)
@@ -177,7 +199,7 @@
         for side, x in ((0, 0), (1, CX - 1)):
             rowsrc[side, 8 * c : 8 * c + 8, :] = vel[pl.ds(c * PZ * CX + x, PZ, stride=CX), :]
         for side, p in ((0, PZ - 1), (1, 0)):
-            zsrc[side, c * CX : (c + 1) * CX, :] = vel[pl.ds((c * PZ + p) * CX, CX), :]
+            zsrc[(side * 3 + c) * CX : (side * 3 + c + 1) * CX, :] = vel[pl.ds((c * PZ + p) * CX, CX), :]
     lane = lanes((CX, CY))
 
     def pack_cols(p, acc):
@@ -189,51 +211,31 @@
 
     colsrc[...] = lax.fori_loop(0, PZ, pack_cols, jnp.zeros((CX, CY), f32))
 
-    def halo_copies():
-        out = []
-        for d in (-1, 0, 1):
-            for side, to_x in ((0, up_x), (1, down_x)):
-                slot = 1 - d
-                out.append(
-                    pltpu.make_async_remote_copy(
-                        src_ref=rowsrc.at[1 - side],
-                        dst_ref=rowdst.at[side, slot],
-                        send_sem=hs.at[side * 3 + slot],
-                        recv_sem=hrv.at[side * 3 + slot],
-                        device_id=(to_x, ys[1 + d], igr),
-                        device_id_type=MESH,
-                    )
-                )
-        for side, to_y in ((0, ys[2]), (1, ys[0])):
-            out.append(
-                pltpu.make_async_remote_copy(
-                    src_ref=colsrc,
-                    dst_ref=coldst.at[side],
-                    send_sem=hs.at[6 + side],
-                    recv_sem=hrv.at[6 + side],
-                    device_id=(isx, to_y, igr),
-                    device_id_type=MESH,
+    halo = []
+    for d in (-1, 0, 1):
+        for side, to_x in ((0, up_x), (1, down_x)):
+            slot = side * 3 + 1 - d
+            halo.append(
+                remote(
+                    rowsrc.at[1 - side], hdst.at[pl.ds(slot * 24, 24)],
+                    hs.at[0], hrv.at[0], (to_x, ys[1 + d], igr),
                 )
             )
-        for side in (0, 1):
-            out.append(
-                pltpu.make_async_remote_copy(
-                    src_ref=zsrc.at[side],
-                    dst_ref=zdst.at[side],
-                    send_sem=hs.at[8 + side],
-                    recv_sem=hrv.at[8 + side],
-                    device_id=(isx, isy, other),
-                    device_id_type=MESH,
-                )
+    for side, to_y in ((0, ys[2]), (1, ys[0])):
+        halo.append(
+            remote(
+                colsrc, hdst.at[pl.ds(144 + side * CX, CX)],
+                hs.at[0], hrv.at[0], (isx, to_y, igr),
             )
-        return out
-
-    halo = halo_copies()
+        )
+    halo_all = all_of(hdst, hs.at[0], hrv.at[0])
+    halo_z = remote(zsrc, zdst, hs.at[1], hrv.at[1], (isx, isy, other))
 
     def enter():
-        pl.semaphore_wait(barrier, (n_sy - 1) + (n_b - 1) + 4)
+        pl.semaphore_wait(barrier, len(friends))
         for copy in halo:
             copy.start()
+        halo_z.start()
 
     loads[1].wait()
     names = tmap[...]
@@ -324,78 +326,71 @@
     grad[0:128, :] = grad[0:128, :] * (0.5 / lam)
     grad[176:184, :] = grad[176:184, :] * (0.5 / lam)
 
-    seg = GROWS // n_sy
-    for j in range(n_sy):
-        gseg[j] = grad[j * seg : (j + 1) * seg, :]
-
-    def a_copy(k):
-        to = lax.rem(isy + k, n_sy)
-        return pltpu.make_async_remote_copy(
-            src_ref=gseg.at[to], dst_ref=ra.at[isy],
-            send_sem=a_s.at[to], recv_sem=a_r.at[isy],
-            device_id=(isx, to, igr), device_id_type=MESH,
-        )
-
-    def a_arrival(k):
-        of = lax.rem(isy + k, n_sy)
-        return pltpu.make_async_remote_copy(
-            src_ref=gseg.at[of], dst_ref=ra.at[of],
-            send_sem=a_s.at[of], recv_sem=a_r.at[of],
-            device_id=(isx, of, igr), device_id_type=MESH,
-        )
-
-    def b_copy(k, mine):
-        at = lax.rem(ib + k, n_b)
-        of = ib if mine else at
-        return pltpu.make_async_remote_copy(
-            src_ref=sb_sum, dst_ref=rb.at[of],
-            send_sem=b_s.at[at], recv_sem=b_r.at[of],
-            device_id=(at // n_grp, isy, lax.rem(at, n_grp)), device_id_type=MESH,
-        )
-
-    def c_copy(k, mine):
-        at = lax.rem(isy + k, n_sy)
-        of = isy if mine else at
-        return pltpu.make_async_remote_copy(
-            src_ref=fin, dst_ref=rc.at[of],
-            send_sem=c_s.at[at], recv_sem=c_r.at[of],
-            device_id=(isx, at, igr), device_id_type=MESH,
-        )
-
-    def each(count, act):
-        def step(k, _):
-            act(k)
-            return 0
-
-        lax.fori_loop(1, count, step, 0)
-
-    ra[isy] = gseg[isy]
-    each(n_sy, lambda k: a_copy(k).start())
+    seg = GROWS // n_sx
+
+    def seg_at(i):
+        return pl.ds(pl.multiple_of(i * seg, 8), seg)
+
+    scatter = [
+        remote(grad.at[seg_at(in_sx(k))], ra.at[isx], rs.at[0], rr.at[0], at_sx(in_sx(k)))
+        for k in range(1, n_sx)
+    ]
+    scatter_all = all_of(ra.at[pl.ds(0, n_sx - 1)], rs.at[0], rr.at[0])
+    near = [
+        remote(part_a, rb.at[low], rs.at[1], rr.at[1], at_low(in_low(k)))
+        for k in range(1, n_low)
+    ]
+    near_all = all_of(rb.at[pl.ds(0, n_low - 1)], rs.at[1], rr.at[1])
+    wide = [
+        remote(part_b, rc.at[far], rs.at[2], rr.at[2], at_far(in_far(k)))
+        for k in range(1, n_far)
+    ]
+    wide_all = all_of(rc.at[pl.ds(0, n_far - 1)], rs.at[2], rr.at[2])
+    gather = [
+        remote(part_c, rd.at[isx], rs.at[3], rr.at[3], at_sx(in_sx(k)))
+        for k in range(1, n_sx)
+    ]
+    gather_all = all_of(rd.at[pl.ds(0, n_sx - 1)], rs.at[3], rr.at[3])
+
+    def total_of(buffer, count):
+        total = buffer[0]
+        for j in range(1, count):
+            total = total + buffer[j]
+        return total
+
+    ra[isx] = grad[seg_at(isx), :]
+    for copy in scatter:
+        copy.start()
 
     def second():
-        each(n_sy, lambda k: a_arrival(k).wait_recv())
-        total = ra[0]
-        for j in range(1, n_sy):
-            total = total + ra[j]
-        sb_sum[...] = total
-        rb[ib] = total
-        each(n_b, lambda k: b_copy(k, True).start())
+        scatter_all.wait_recv()
+        total = total_of(ra, n_sx)
+        part_a[...] = total
+        rb[low] = total
+        for copy in near:
+            copy.start()
 
     def third():
-        each(n_b, lambda k: b_copy(k, False).wait_recv())
-        total = rb[0]
-        for j in range(1, n_b):
-            total = total + rb[j]
-        fin[...] = total
-        rc[isy] = total
-        each(n_sy, lambda k: c_copy(k, True).start())
+        near_all.wait_recv()
+        total = total_of(rb, n_low)
+        part_b[...] = total
+        rc[far] = total
+        for copy in wide:
+            copy.start()
+
+    def fourth():
+        wide_all.wait_recv()
+        total = total_of(rc, n_far)
+        part_c[...] = total
+        rd[isx] = total
+        for copy in gather:
+            copy.start()
 
     qf[...] = jnp.ones(qf.shape, f32)
-    for copy in halo[0:8]:
-        copy.wait_recv()
+    halo_all.wait_recv()
     lane24 = lanes((24, CY))
     for side in (0, 1):
-        left, mid, right = rowdst[side, 0], rowdst[side, 1], rowdst[side, 2]
+        left, mid, right = (hdst[(side * 3 + i) * 24 : (side * 3 + i + 1) * 24, :] for i in range(3))
         shifted = (
             jnp.where(lane24 == 0, pltpu.roll(left, 1, 1), pltpu.roll(mid, 1, 1)),
             mid,
@@ -409,7 +404,7 @@
             for c in range(3):
                 qf[pl.ds(at + c * 3 + b, PZ, stride=PLANE), :] = hr[8 * c : 8 * c + 8, :]
     cc[...] = jnp.where(
-        lax.rem(lane, 2) == 0, pltpu.roll(coldst[1], CY - 1, 1), pltpu.roll(coldst[0], 1, 1)
+        lax.rem(lane, 2) == 0, pltpu.roll(hdst[176:208, :], CY - 1, 1), pltpu.roll(hdst[144:176, :], 1, 1)
     )
 
     def build(p):
@@ -445,53 +440,37 @@
         for x in range(XC):
             stress[at + x * TROW : at + (x + 1) * TROW, :] = tau[:, x * CY : (x + 1) * CY]
 
-    def z_copies():
-        out = []
-        for side, p in ((0, PZ), (1, 1)):
-            out.append(
-                pltpu.make_async_remote_copy(
-                    src_ref=stress.at[pl.ds(p * TPLANE + TROW, CX * TROW)],
-                    dst_ref=stress.at[pl.ds((PZ + 1) * side * TPLANE + TROW, CX * TROW)],
-                    send_sem=ss.at[side],
-                    recv_sem=srv.at[side],
-                    device_id=(isx, isy, other),
-                    device_id_type=MESH,
-                )
-            )
-        return out
-
-    zs = z_copies()
+    zs = [
+        remote(
+            stress.at[pl.ds(p * TPLANE + TROW, CX * TROW)],
+            stress.at[pl.ds((PZ + 1) * side * TPLANE + TROW, CX * TROW)],
+            ss.at[2], srv.at[2], (isx, isy, other),
+        )
+        for side, p in ((0, PZ), (1, 1))
+    ]
+    zs_all = all_of(stress.at[pl.ds(0, 2 * CX * TROW)], ss.at[2], srv.at[2])
 
     scolsrc[...] = jnp.zeros(scolsrc.shape, f32)
     srowsrc[...] = jnp.zeros(srowsrc.shape, f32)
 
     def edge_copies(group):
-        out = []
-        for side, to_x in ((0, up_x), (1, down_x)):
-            out.append(
-                pltpu.make_async_remote_copy(
-                    src_ref=srowsrc.at[group, 1 - side],
-                    dst_ref=srowdst.at[group, side],
-                    send_sem=ss.at[2 + 4 * group + side],
-                    recv_sem=srv.at[2 + 4 * group + side],
-                    device_id=(to_x, isy, igr),
-                    device_id_type=MESH,
-                )
+        out = [
+            remote(
+                srowsrc.at[group, 1 - side], edst.at[group, pl.ds(side * 24, 24)],
+                ss.at[group], srv.at[group], (to_x, isy, igr),
             )
-        for side, to_y in ((0, ys[2]), (1, ys[0])):
-            out.append(
-                pltpu.make_async_remote_copy(
-                    src_ref=scolsrc.at[group],
-                    dst_ref=scoldst.at[group, side],
-                    send_sem=ss.at[4 + 4 * group + side],
-                    recv_sem=srv.at[4 + 4 * group + side],
-                    device_id=(isx, to_y, igr),
-                    device_id_type=MESH,
-                )
+            for side, to_x in ((0, up_x), (1, down_x))
+        ]
+        return out + [
+            remote(
+                scolsrc.at[group], edst.at[group, pl.ds(48 + side * CX, CX)],
+                ss.at[group], srv.at[group], (isx, to_y, igr),
             )
-        return out
+            for side, to_y in ((0, ys[2]), (1, ys[0]))
+        ]
 
     edges = [edge_copies(0), edge_copies(1)]
+    edges_all = [all_of(edst.at[g], ss.at[g], srv.at[g]) for g in (0, 1)]
     groups = (ORDER[:EARLY], ORDER[EARLY:])
 
     def send_edges(group):
@@ -526,14 +505,15 @@
                 copy.start()
         if k - 2 == EARLY * PER - 1:
             send_edges(0)
-        if k == 8:
+        if k == 6:
             second()
-        if k == 14:
+        if k == 9:
             third()
+        if k == 13:
+            fourth()
     send_edges(1)
 
-    for copy in halo[8:10]:
-        copy.wait_recv()
+    halo_z.wait_recv()
 
     def viscous(p, below, above):
         for c in range(3):
@@ -552,7 +532,7 @@
         return lambda c: vel[pl.ds(pl.multiple_of((c * PZ + p) * CX, CX), CX), :]
 
     def ghost(side):
-        return lambda c: zdst[side, c * CX : (c + 1) * CX, :]
+        return lambda c: zdst[(side * 3 + c) * CX : (side * 3 + c + 1) * CX, :]
 
     viscous(0, ghost(0), plane_of(1))
 
@@ -563,9 +543,10 @@
     lax.fori_loop(1, PZ - 1, inner, 0)
     viscous(PZ - 1, plane_of(PZ - 2), ghost(1))
 
-    each(n_sy, lambda k: c_copy(k, False).wait_recv())
-    for j in range(n_sy):
-        grad[j * seg : (j + 1) * seg, :] = rc[j]
+    gather_all.wait_recv()
+    scatter_all.wait_send()
+    for j in range(n_sx):
+        grad[j * seg : (j + 1) * seg, :] = rd[j]
     gmix[...] = grad[0:128, :]
     for c in range(3):
         for a in range(3):
@@ -594,30 +575,27 @@
             at = pl.ds(j * CX, CX)
             tend[at, :] = tend[at, :] - half * (along_x + along_y + along_z)
 
-    for copy in zs:
-        copy.wait_send()
-        copy.wait_recv()
+    zs_all.wait_send()
+    zs_all.wait_recv()
     for group in (0, 1):
-        for copy in edges[group]:
-            copy.wait_recv()
+        edges_all[group].wait_recv()
         for p in groups[group]:
             for side in (0, 1):
                 for c in range(3):
                     at = (p + 1) * TPLANE + side * (CX + 1) * TROW + DX[c]
-                    stress[at : at + 1, :] = srowdst[group, side, c * PZ + p : c * PZ + p + 1, :]
+                    stress[at : at + 1, :] = edst[
+                        group, side * 24 + c * PZ + p : side * 24 + c * PZ + p + 1, :
+                    ]
         scc[...] = jnp.where(
             lax.rem(lane, 2) == 0,
-            pltpu.roll(scoldst[group, 1], CY - 1, 1),
-            pltpu.roll(scoldst[group, 0], 1, 1),
+            pltpu.roll(edst[group, 80:112, :], CY - 1, 1),
+            pltpu.roll(edst[group, 48:80, :], 1, 1),
         )
         for p in groups[group]:
             diverge(p)
 
-    for copy in halo + edges[0] + edges[1]:
-        copy.wait_send()
-    each(n_sy, lambda k: a_copy(k).wait_send())
-    each(n_b, lambda k: b_copy(k, True).wait_send())
-    each(n_sy, lambda k: c_copy(k, True).wait_send())
+    for group in (halo_all, halo_z, *edges_all, near_all, wide_all, gather_all):
+        group.wait_send()
 
 
 def write_out(*refs):
@@ -627,8 +605,9 @@
 
 def shards(velocity, target_stress, w_conv, b_conv, w_mix, b_mix, w_out, plane_offsets, trainer_map):
     n_sx, n_sy, n_grp = (lax.axis_size(a) for a in ("sx", "sy", "grp"))
-    n_b = n_sx * n_grp
-    seg = GROWS // n_sy
+    n_low = min(4, n_sy)
+    n_far = n_sy // n_low * n_grp
+    seg = GROWS // n_sx
     gscale = 1.0 / math.sqrt(S * n_sx * n_sy * n_grp * CX * CY)
     vmem = pl.BlockSpec(memory_space=pltpu.VMEM)
     smem = pl.BlockSpec(memory_space=pltpu.SMEM)
@@ -665,15 +644,15 @@
             buf(2, 128, NC, dtype=bf16), buf(2, 128, NC, dtype=bf16), buf(2, 8, NC),
             buf(GROWS, 128),
             *[buf(S * PER, 128, NC, dtype=bf16) for _ in range(5)],
-            buf(2, 24, CY), buf(2, 3, 24, CY), buf(CX, CY), buf(2, CX, CY),
-            buf(2, 3 * CX, CY), buf(2, 3 * CX, CY),
+            buf(2, 24, CY), buf(CX, CY), buf(208, CY),
+            buf(6 * CX, CY), buf(6 * CX, CY),
             buf(24, CY), buf(CX, CY),
-            buf(2, 2, 24, CY), buf(2, 2, 24, CY), buf(2, CX, CY), buf(2, 2, CX, CY), buf(CX, CY),
-            buf(n_sy, seg, 128), buf(n_sy, seg, 128),
-            buf(seg, 128), buf(n_b, seg, 128),
-            buf(seg, 128), buf(n_sy, seg, 128),
-            sems(2), sems(10), sems(10), sems(10), sems(10),
-            sems(n_sy), sems(n_sy), sems(n_b), sems(n_b), sems(n_sy), sems(n_sy),
+            buf(2, 2, 24, CY), buf(2, CX, CY), buf(2, 112, CY), buf(CX, CY),
+            buf(n_sx, seg, 128), buf(seg, 128),
+            buf(n_low, seg, 128), buf(seg, 128),
+            buf(n_far, seg, 128), buf(seg, 128),
+            buf(n_sx, seg, 128),
+            sems(2), sems(2), sems(2), sems(3), sems(3), sems(4), sems(4),
         ],
         compiler_params=pltpu.CompilerParams(
             collective_id=0, has_side_effects=True, vmem_limit_bytes=62 * 2**20

time: 39.3 us -> 41.3 us (1.051)
  Pallas kernels: 38.5 us -> 40.5 us
    pallas_call x1, Pallas kernels: 36.7 us -> 38.7 us  [shards(): pl.pallas_call(functools.partial(kernel, n_sx, n_sy, n_grp, gscale), out_...]
where the time goes in v3:
time: 41.3 us; the launch traced here: 41.2 us
  Pallas kernels  40.5 us (98%)
  between operations  0.64 us (2%)
    pallas_call x1, Pallas kernels, shards(): pl.pallas_call(functools.partial(kernel, n_sx, n_sy, n_grp, gscale), out_...  38.7 us
    pallas_call x1, Pallas kernels, shards(): pl.pallas_call(write_out, out_shape=[jax.ShapeDtypeStruct(o.shape, o.dtyp...  1.85 us

profile of v3, /device:TPU:1, one launch (start us, length us, event | category | flops | bytes accessed | tf_op | source)
XLA Modules:
  0.0 41.2 jit_solution(13364913737447579053)
XLA Ops:
  0.6 38.7 %shard_map.136 = (f32[768,128]{1,0:T(8,128)}, f32[27,128]{1,0:T(8,128)}, f32[1,128]{1,0:T(1,128)}, f32[128,128]{1,0:T(8,128)}, f32[1,128]{1,0:T(1,128)}, /*index=5*/f32[6,128]{1,0:T(8,128)}) custom-call(f32[768,128]{1,0:T(8,128)} %bitcast.12, f32[1536,128]{1,0:T(8,128)} %bitcast.11, bf16[27,128]{1,0:T(8,128)(2,1)} %wc.1, f32[1,128]{1,0:T(1,128)} %bitcast.14, ...), custom_call_target="tpu_custom_call" | custom-call | tf_op jit(solution)/shard_map/pallas_call | solution.py:622
  39.3 1.8 %shard_map.137 = (f32[768,128]{1,0:T(8,128)}, f32[27,128]{1,0:T(8,128)}, f32[1,128]{1,0:T(1,128)}, f32[128,128]{1,0:T(8,128)}, f32[1,128]{1,0:T(1,128)}, /*index=5*/f32[6,128]{1,0:T(8,128)}) custom-call(f32[768,128]{1,0:T(8,128)} %get-tuple-element.18.refs_0_, f32[27,128]{1,0:T(8,128)} %get-tuple-element.19.refs_1_, f32[1,128]{1,0:T(1,128)} %get-tuple-element.20.refs_2_, ...), custom_call_target="tpu_custom_call" | custom-call | tf_op jit(solution)/shard_map/pallas_call | solution.py:671

commit v4 on v3

--- a/solution.py
+++ b/solution.py
@@ -93,36 +93,28 @@
     qf, qb, sf, sb, tg, stress, cw, mw, ow, tw2, wb2, wbo, prep, prep2,
     q1, q2, lin, grad, h1, d1, h2, d2, g2,
     rowsrc, colsrc, hdst, zsrc, zdst, hr, cc,
-    srowsrc, scolsrc, edst, scc,
-    ra, part_a, rb, part_b, rc, part_c, rd,
+    srowsrc, scolsrc, edst, scc, szsrc, szdst,
+    gseg, ra, part_a, rb, part_b, rc,
     ins, hs, hrv, ss, srv, rs, rr,
 ):
     isx, isy, igr = lax.axis_index("sx"), lax.axis_index("sy"), lax.axis_index("grp")
     up_x, down_x = lax.rem(isx + 1, n_sx), lax.rem(isx + n_sx - 1, n_sx)
     ys = (lax.rem(isy + n_sy - 1, n_sy), isy, lax.rem(isy + 1, n_sy))
     other = 1 - igr
-    n_low = min(4, n_sy)
-    n_far = n_sy // n_low * n_grp
-    low, high = lax.rem(isy, n_low), isy // n_low
-    far = high * n_grp + igr
-
-    def in_sx(k):
-        return lax.rem(isx + k, n_sx)
-
-    def in_low(k):
-        return lax.rem(low + k, n_low)
-
-    def in_far(k):
-        return lax.rem(far + k, n_far)
-
-    def at_sx(i):
-        return (i, isy, igr)
-
-    def at_low(i):
-        return (isx, high * n_low + i, igr)
-
-    def at_far(i):
-        return (isx, i // n_grp * n_low + low, lax.rem(i, n_grp))
+    n_b = n_sx * n_grp
+    ib = isx * n_grp + igr
+
+    def in_sy(k):
+        return lax.rem(isy + k, n_sy)
+
+    def in_b(k):
+        return lax.rem(ib + k, n_b)
+
+    def at_sy(i):
+        return (isx, i, igr)
+
+    def at_b(i):
+        return (i // n_grp, isy, lax.rem(i, n_grp))
 
     loads = [
         pltpu.make_async_copy(vel_in, vel, ins.at[0]),
@@ -136,10 +128,8 @@
     def greet(device):
         pl.semaphore_signal(barrier, inc=1, device_id=device, device_id_type=MESH)
 
-    friends = [at_sx(in_sx(k)) for k in range(1, n_sx)]
-    friends += [at_low(in_low(k)) for k in range(1, n_low)]
-    friends += [at_far(in_far(k)) for k in range(1, n_far)]
-    friends += [(isx, ys[0], igr), (isx, ys[2], igr)]
+    friends = [at_sy(in_sy(k)) for k in range(1, n_sy)]
+    friends += [at_b(in_b(k)) for k in range(1, n_b)]
     friends += [(to_x, to_y, igr) for to_x in (up_x, down_x) for to_y in (ys[0], ys[2])]
     for device in friends:
         greet(device)
@@ -151,7 +141,7 @@
         )
 
     def all_of(buffer, send, recv):
-        return remote(buffer, buffer, send, recv, at_sx(in_sx(1)))
+        return remote(buffer, buffer, send, recv, at_sy(in_sy(1)))
 
     prep[...] = jnp.zeros(prep.shape, f32)
     for c in range(3):
@@ -326,31 +316,22 @@
     grad[0:128, :] = grad[0:128, :] * (0.5 / lam)
     grad[176:184, :] = grad[176:184, :] * (0.5 / lam)
 
-    seg = GROWS // n_sx
-
-    def seg_at(i):
-        return pl.ds(pl.multiple_of(i * seg, 8), seg)
-
+    seg = GROWS // n_sy
+    for j in range(n_sy):
+        gseg[j] = grad[j * seg : (j + 1) * seg, :]
     scatter = [
-        remote(grad.at[seg_at(in_sx(k))], ra.at[isx], rs.at[0], rr.at[0], at_sx(in_sx(k)))
-        for k in range(1, n_sx)
+        remote(gseg.at[in_sy(k)], ra.at[isy], rs.at[0], rr.at[0], at_sy(in_sy(k)))
+        for k in range(1, n_sy)
     ]
-    scatter_all = all_of(ra.at[pl.ds(0, n_sx - 1)], rs.at[0], rr.at[0])
-    near = [
-        remote(part_a, rb.at[low], rs.at[1], rr.at[1], at_low(in_low(k)))
-        for k in range(1, n_low)
+    scatter_all = all_of(ra.at[pl.ds(0, n_sy - 1)], rs.at[0], rr.at[0])
+    wide = [
+        remote(part_a, rb.at[ib], rs.at[1], rr.at[1], at_b(in_b(k))) for k in range(1, n_b)
     ]
-    near_all = all_of(rb.at[pl.ds(0, n_low - 1)], rs.at[1], rr.at[1])
-    wide = [
-        remote(part_b, rc.at[far], rs.at[2], rr.at[2], at_far(in_far(k)))
-        for k in range(1, n_far)
+    wide_all = all_of(rb.at[pl.ds(0, n_b - 1)], rs.at[1], rr.at[1])
+    gather = [
+        remote(part_b, rc.at[isy], rs.at[2], rr.at[2], at_sy(in_sy(k))) for k in range(1, n_sy)
     ]
-    wide_all = all_of(rc.at[pl.ds(0, n_far - 1)], rs.at[2], rr.at[2])
-    gather = [
-        remote(part_c, rd.at[isx], rs.at[3], rr.at[3], at_sx(in_sx(k)))
-        for k in range(1, n_sx)
-    ]
-    gather_all = all_of(rd.at[pl.ds(0, n_sx - 1)], rs.at[3], rr.at[3])
+    gather_all = all_of(rc.at[pl.ds(0, n_sy - 1)], rs.at[2], rr.at[2])
 
     def total_of(buffer, count):
         total = buffer[0]
@@ -358,31 +339,23 @@
             total = total + buffer[j]
         return total
 
-    ra[isx] = grad[seg_at(isx), :]
+    ra[isy] = gseg[isy]
     for copy in scatter:
         copy.start()
 
     def second():
         scatter_all.wait_recv()
-        total = total_of(ra, n_sx)
+        total = total_of(ra, n_sy)
         part_a[...] = total
-        rb[low] = total
-        for copy in near:
-            copy.start()
-
-    def third():
-        near_all.wait_recv()
-        total = total_of(rb, n_low)
-        part_b[...] = total
-        rc[far] = total
+        rb[ib] = total
         for copy in wide:
             copy.start()
 
-    def fourth():
+    def third():
         wide_all.wait_recv()
-        total = total_of(rc, n_far)
-        part_c[...] = total
-        rd[isx] = total
+        total = total_of(rb, n_b)
+        part_b[...] = total
+        rc[isy] = total
         for copy in gather:
             copy.start()
 
@@ -436,19 +409,20 @@
 
     def stage_out(k):
         tau = dot(ow[...], q2[k % 2])[0:8] + lin[k % 2]
-        at = (ORDER[k // PER] + 1) * TPLANE + (k % PER * XC + 1) * TROW
+        at = ORDER[k // PER] * TPLANE + (k % PER * XC + 1) * TROW
         for x in range(XC):
             stress[at + x * TROW : at + (x + 1) * TROW, :] = tau[:, x * CY : (x + 1) * CY]
 
-    zs = [
-        remote(
-            stress.at[pl.ds(p * TPLANE + TROW, CX * TROW)],
-            stress.at[pl.ds((PZ + 1) * side * TPLANE + TROW, CX * TROW)],
-            ss.at[2], srv.at[2], (isx, isy, other),
-        )
-        for side, p in ((0, PZ), (1, 1))
-    ]
-    zs_all = all_of(stress.at[pl.ds(0, 2 * CX * TROW)], ss.at[2], srv.at[2])
+    zs = remote(szsrc, szdst, ss.at[2], srv.at[2], (isx, isy, other))
+
+    def send_z():
+        for side, p in ((0, PZ - 1), (1, 0)):
+            for c in range(3):
+                at = (side * 3 + c) * CX
+                szsrc[at : at + CX, :] = stress[
+                    pl.ds(p * TPLANE + TROW + DZ[c], CX, stride=TROW), :
+                ]
+        zs.start()
 
     scolsrc[...] = jnp.zeros(scolsrc.shape, f32)
     srowsrc[...] = jnp.zeros(srowsrc.shape, f32)
@@ -478,7 +452,7 @@
         for p in groups[group]:
             for c in range(3):
                 j = c * PZ + p
-                at = (p + 1) * TPLANE
+                at = p * TPLANE
                 for side, x in ((0, 1), (1, CX)):
                     srowsrc[group, side, j : j + 1, :] = stress[
                         at + x * TROW + DX[c] : at + x * TROW + DX[c] + 1, :
@@ -500,17 +474,14 @@
             stage_mix(k - 1)
         if k < chunks:
             stage_conv(k)
-        if k - 2 == 2 * PER - 1:
-            for copy in zs:
-                copy.start()
+        if k == 14:
+            send_z()
         if k - 2 == EARLY * PER - 1:
             send_edges(0)
         if k == 6:
             second()
-        if k == 9:
+        if k == 13:
             third()
-        if k == 13:
-            fourth()
     send_edges(1)
 
     halo_z.wait_recv()
@@ -543,19 +514,6 @@
     lax.fori_loop(1, PZ - 1, inner, 0)
     viscous(PZ - 1, plane_of(PZ - 2), ghost(1))
 
-    gather_all.wait_recv()
-    scatter_all.wait_send()
-    for j in range(n_sx):
-        grad[j * seg : (j + 1) * seg, :] = rd[j]
-    gmix[...] = grad[0:128, :]
-    for c in range(3):
-        for a in range(3):
-            at = 128 + a * BLK + c * 3
-            gconv[c * 9 + 3 * a : c * 9 + 3 * a + 3, :] = grad[at : at + 3, :]
-    gbconv[...] = grad[137:138, :]
-    gbmix[...] = grad[185:186, :]
-    gout[...] = grad[176:182, :]
-
     half = 0.25 / lam
 
     def diverge(p):
@@ -563,26 +521,28 @@
             j = c * PZ + p
 
             def pick_at(plane, x, comp):
-                return stress[pl.ds((p + plane) * TPLANE + x * TROW + comp, CX, stride=TROW), :]
-
-            along_x = pick_at(1, 2, DX[c]) - pick_at(1, 0, DX[c])
-            v = pick_at(1, 1, DY[c])
+                if plane < 0 or plane == PZ:
+                    side = 0 if plane < 0 else 1
+                    return szdst[(side * 3 + c) * CX : (side * 3 + c + 1) * CX, :]
+                return stress[pl.ds(plane * TPLANE + x * TROW + comp, CX, stride=TROW), :]
+
+            along_x = pick_at(p, 2, DX[c]) - pick_at(p, 0, DX[c])
+            v = pick_at(p, 1, DY[c])
             edge = pltpu.roll(scc[...], CY - 1 - 2 * j, 1)
             along_y = jnp.where(lane == CY - 1, edge, pltpu.roll(v, CY - 1, 1)) - jnp.where(
                 lane == 0, edge, pltpu.roll(v, 1, 1)
             )
-            along_z = pick_at(2, 1, DZ[c]) - pick_at(0, 1, DZ[c])
+            along_z = pick_at(p + 1, 1, DZ[c]) - pick_at(p - 1, 1, DZ[c])
             at = pl.ds(j * CX, CX)
             tend[at, :] = tend[at, :] - half * (along_x + along_y + along_z)
 
-    zs_all.wait_send()
-    zs_all.wait_recv()
+    zs.wait_recv()
     for group in (0, 1):
         edges_all[group].wait_recv()
         for p in groups[group]:
             for side in (0, 1):
                 for c in range(3):
-                    at = (p + 1) * TPLANE + side * (CX + 1) * TROW + DX[c]
+                    at = p * TPLANE + side * (CX + 1) * TROW + DX[c]
                     stress[at : at + 1, :] = edst[
                         group, side * 24 + c * PZ + p : side * 24 + c * PZ + p + 1, :
                     ]
@@ -594,7 +554,19 @@
         for p in groups[group]:
             diverge(p)
 
-    for group in (halo_all, halo_z, *edges_all, near_all, wide_all, gather_all):
+    gather_all.wait_recv()
+    for j in range(n_sy):
+        grad[j * seg : (j + 1) * seg, :] = rc[j]
+    gmix[...] = grad[0:128, :]
+    for c in range(3):
+        for a in range(3):
+            at = 128 + a * BLK + c * 3
+            gconv[c * 9 + 3 * a : c * 9 + 3 * a + 3, :] = grad[at : at + 3, :]
+    gbconv[...] = grad[137:138, :]
+    gbmix[...] = grad[185:186, :]
+    gout[...] = grad[176:182, :]
+
+    for group in (halo_all, halo_z, zs, *edges_all, scatter_all, wide_all, gather_all):
         group.wait_send()
 
 
@@ -605,9 +577,8 @@
 
 def shards(velocity, target_stress, w_conv, b_conv, w_mix, b_mix, w_out, plane_offsets, trainer_map):
     n_sx, n_sy, n_grp = (lax.axis_size(a) for a in ("sx", "sy", "grp"))
-    n_low = min(4, n_sy)
-    n_far = n_sy // n_low * n_grp
-    seg = GROWS // n_sx
+    n_b = n_sx * n_grp
+    seg = GROWS // n_sy
     gscale = 1.0 / math.sqrt(S * n_sx * n_sy * n_grp * CX * CY)
     vmem = pl.BlockSpec(memory_space=pltpu.VMEM)
     smem = pl.BlockSpec(memory_space=pltpu.SMEM)
@@ -636,7 +607,7 @@
             buf(PZ * PLANE, CY), buf(PZ * PLANE, CY, dtype=bf16),
             buf(S * PLANE, CY), buf(S * PLANE, CY, dtype=bf16),
             buf(S * CX * TROW, CY),
-            buf((PZ + 2) * TPLANE, CY),
+            buf(PZ * TPLANE, CY),
             buf(128, 128, dtype=bf16), buf(144, 256, dtype=bf16), buf(16, 128, dtype=bf16),
             buf(128, 256, dtype=bf16),
             buf(128, 128, dtype=bf16), buf(128, 16, dtype=bf16),
@@ -648,11 +619,10 @@
             buf(6 * CX, CY), buf(6 * CX, CY),
             buf(24, CY), buf(CX, CY),
             buf(2, 2, 24, CY), buf(2, CX, CY), buf(2, 112, CY), buf(CX, CY),
-            buf(n_sx, seg, 128), buf(seg, 128),
-            buf(n_low, seg, 128), buf(seg, 128),
-            buf(n_far, seg, 128), buf(seg, 128),
-            buf(n_sx, seg, 128),
-            sems(2), sems(2), sems(2), sems(3), sems(3), sems(4), sems(4),
+            buf(6 * CX, CY), buf(6 * CX, CY),
+            buf(n_sy, seg, 128), buf(n_sy, seg, 128), buf(seg, 128),
+            buf(n_b, seg, 128), buf(seg, 128), buf(n_sy, seg, 128),
+            sems(2), sems(2), sems(2), sems(3), sems(3), sems(3), sems(3),
         ],
         compiler_params=pltpu.CompilerParams(
             collective_id=0, has_side_effects=True, vmem_limit_bytes=62 * 2**20

time: 41.3 us -> 35.5 us (0.86)
  Pallas kernels: 40.5 us -> 34.7 us
    pallas_call x1, Pallas kernels: 38.7 us -> 32.9 us  [shards(): pl.pallas_call(functools.partial(kernel, n_sx, n_sy, n_grp, gscale), out_...]
where the time goes in v4:
time: 35.5 us; the launch traced here: 35.4 us
  Pallas kernels  34.7 us (98%)
  between operations  0.64 us (2%)
    pallas_call x1, Pallas kernels, shards(): pl.pallas_call(functools.partial(kernel, n_sx, n_sy, n_grp, gscale), out_...  32.9 us
    pallas_call x1, Pallas kernels, shards(): pl.pallas_call(write_out, out_shape=[jax.ShapeDtypeStruct(o.shape, o.dtyp...  1.85 us

profile of v4, /device:TPU:1, one launch (start us, length us, event | category | flops | bytes accessed | tf_op | source)
XLA Modules:
  0.0 35.4 jit_solution(1759649918217014557)
XLA Ops:
  0.6 32.9 %shard_map.136 = (f32[768,128]{1,0:T(8,128)}, f32[27,128]{1,0:T(8,128)}, f32[1,128]{1,0:T(1,128)}, f32[128,128]{1,0:T(8,128)}, f32[1,128]{1,0:T(1,128)}, /*index=5*/f32[6,128]{1,0:T(8,128)}) custom-call(f32[768,128]{1,0:T(8,128)} %bitcast.12, f32[1536,128]{1,0:T(8,128)} %bitcast.11, bf16[27,128]{1,0:T(8,128)(2,1)} %wc.1, f32[1,128]{1,0:T(1,128)} %bitcast.14, ...), custom_call_target="tpu_custom_call" | custom-call | tf_op jit(solution)/shard_map/pallas_call | solution.py:593
  33.5 1.8 %shard_map.137 = (f32[768,128]{1,0:T(8,128)}, f32[27,128]{1,0:T(8,128)}, f32[1,128]{1,0:T(1,128)}, f32[128,128]{1,0:T(8,128)}, f32[1,128]{1,0:T(1,128)}, /*index=5*/f32[6,128]{1,0:T(8,128)}) custom-call(f32[768,128]{1,0:T(8,128)} %get-tuple-element.18.refs_0_, f32[27,128]{1,0:T(8,128)} %get-tuple-element.19.refs_1_, f32[1,128]{1,0:T(1,128)} %get-tuple-element.20.refs_2_, ...), custom_call_target="tpu_custom_call" | custom-call | tf_op jit(solution)/shard_map/pallas_call | solution.py:641

commit v5 on v4

--- a/solution.py
+++ b/solution.py
@@ -56,6 +56,11 @@
 
 def gate(m):
     return (m * jnp.tanh(m * (m * m + shift_c))).astype(bf16)
+
+
+def gate_16(m):
+    m = m.astype(bf16)
+    return m * jnp.tanh(m * (m * m + bf16(shift_c)))
 
 
 def gate_and_slope(m):
@@ -184,6 +189,13 @@
     wb2[...] = w2h.astype(bf16)
     wbo[...] = (0.5 * jnp.where(lanes((128, 16)) < 8, wo16, 0.0)).astype(bf16)
 
+
+    qf[...] = jnp.ones(qf.shape, f32)
+    sf[...] = jnp.ones(sf.shape, f32)
+    tg[...] = jnp.zeros(tg.shape, f32)
+    grad[...] = jnp.zeros(grad.shape, f32)
+    scolsrc[...] = jnp.zeros(scolsrc.shape, f32)
+    srowsrc[...] = jnp.zeros(srowsrc.shape, f32)
     loads[0].wait()
     for c in range(3):
         for side, x in ((0, 0), (1, CX - 1)):
@@ -238,9 +250,7 @@
 
     scales = [scale_of(s) for s in range(S)]
 
-    sf[...] = jnp.ones(sf.shape, f32)
     zero8 = jnp.zeros((8, 128), f32)
-    tg[...] = jnp.zeros(tg.shape, f32)
     for s in range(S):
         chosen = lax.broadcasted_iota(jnp.int32, (PZ, CX, CY), 0) == offs[s]
 
@@ -265,7 +275,6 @@
         for c in range(6):
             tg[pl.ds(s * CX * TROW + c, CX, stride=TROW), :] = scales[s] * plane(tgt, c)
     sb[...] = sf[...].astype(bf16)
-    grad[...] = jnp.zeros(grad.shape, f32)
 
     def sample_patches(k):
         s, part = k // PER, k % PER
@@ -359,7 +368,6 @@
         for copy in gather:
             copy.start()
 
-    qf[...] = jnp.ones(qf.shape, f32)
     halo_all.wait_recv()
     lane24 = lanes((24, CY))
     for side in (0, 1):
@@ -399,7 +407,7 @@
 
     def stage_conv(k):
         pats = patches_of(k)
-        q1[k % 2] = gate(dot(cw[:, 0:96], jnp.concatenate([pats, pats], axis=0)))
+        q1[k % 2] = gate_16(dot(cw[:, 0:96], jnp.concatenate([pats, pats], axis=0)))
 
     def stage_mix(k):
         pats = patches_of(k)
@@ -424,8 +432,6 @@
                 ]
         zs.start()
 
-    scolsrc[...] = jnp.zeros(scolsrc.shape, f32)
-    srowsrc[...] = jnp.zeros(srowsrc.shape, f32)
 
     def edge_copies(group):
         out = [

time: 35.5 us -> 35.7 us (level)
  no operation moved by 1% of the time
where the time goes in v5:
time: 35.7 us; the launch traced here: 35.5 us
  Pallas kernels  34.9 us (98%)
  between operations  0.64 us (2%)
    pallas_call x1, Pallas kernels, shards(): pl.pallas_call(functools.partial(kernel, n_sx, n_sy, n_grp, gscale), out_...  33.1 us
    pallas_call x1, Pallas kernels, shards(): pl.pallas_call(write_out, out_shape=[jax.ShapeDtypeStruct(o.shape, o.dtyp...  1.85 us

profile of v5, /device:TPU:1, one launch (start us, length us, event | category | flops | bytes accessed | tf_op | source)
XLA Modules:
  0.0 35.5 jit_solution(8294470872583797059)
XLA Ops:
  0.6 33.1 %shard_map.136 = (f32[768,128]{1,0:T(8,128)}, f32[27,128]{1,0:T(8,128)}, f32[1,128]{1,0:T(1,128)}, f32[128,128]{1,0:T(8,128)}, f32[1,128]{1,0:T(1,128)}, /*index=5*/f32[6,128]{1,0:T(8,128)}) custom-call(f32[768,128]{1,0:T(8,128)} %bitcast.12, f32[1536,128]{1,0:T(8,128)} %bitcast.11, bf16[27,128]{1,0:T(8,128)(2,1)} %wc.1, f32[1,128]{1,0:T(1,128)} %bitcast.14, ...), custom_call_target="tpu_custom_call" | custom-call | tf_op jit(solution)/shard_map/pallas_call | solution.py:599
  33.7 1.8 %shard_map.137 = (f32[768,128]{1,0:T(8,128)}, f32[27,128]{1,0:T(8,128)}, f32[1,128]{1,0:T(1,128)}, f32[128,128]{1,0:T(8,128)}, f32[1,128]{1,0:T(1,128)}, /*index=5*/f32[6,128]{1,0:T(8,128)}) custom-call(f32[768,128]{1,0:T(8,128)} %get-tuple-element.18.refs_0_, f32[27,128]{1,0:T(8,128)} %get-tuple-element.19.refs_1_, f32[1,128]{1,0:T(1,128)} %get-tuple-element.20.refs_2_, ...), custom_call_target="tpu_custom_call" | custom-call | tf_op jit(solution)/shard_map/pallas_call | solution.py:647

commit v6 on v5

--- a/solution.py
+++ b/solution.py
@@ -480,7 +480,7 @@
             stage_mix(k - 1)
         if k < chunks:
             stage_conv(k)
-        if k == 14:
+        if k == 7:
             send_z()
         if k - 2 == EARLY * PER - 1:
             send_edges(0)
@@ -542,7 +542,6 @@
             at = pl.ds(j * CX, CX)
             tend[at, :] = tend[at, :] - half * (along_x + along_y + along_z)
 
-    zs.wait_recv()
     for group in (0, 1):
         edges_all[group].wait_recv()
         for p in groups[group]:
@@ -558,7 +557,12 @@
             pltpu.roll(edst[group, 48:80, :], 1, 1),
         )
         for p in groups[group]:
-            diverge(p)
+            if p not in (0, PZ - 1):
+                diverge(p)
+        if group == 0:
+            zs.wait_recv()
+            diverge(0)
+            diverge(PZ - 1)
 
     gather_all.wait_recv()
     for j in range(n_sy):

time: 35.7 us -> 36 us (level)
  no operation moved by 1% of the time
where the time goes in v6:
time: 36 us; the launch traced here: 35.8 us
  Pallas kernels  35.2 us (98%)
  between operations  0.64 us (2%)
    pallas_call x1, Pallas kernels, shards(): pl.pallas_call(functools.partial(kernel, n_sx, n_sy, n_grp, gscale), out_...  33.3 us
    pallas_call x1, Pallas kernels, shards(): pl.pallas_call(write_out, out_shape=[jax.ShapeDtypeStruct(o.shape, o.dtyp...  1.85 us

profile of v6, /device:TPU:1, one launch (start us, length us, event | category | flops | bytes accessed | tf_op | source)
XLA Modules:
  0.0 35.8 jit_solution(261025343800554888)
XLA Ops:
  0.6 33.3 %shard_map.136 = (f32[768,128]{1,0:T(8,128)}, f32[27,128]{1,0:T(8,128)}, f32[1,128]{1,0:T(1,128)}, f32[128,128]{1,0:T(8,128)}, f32[1,128]{1,0:T(1,128)}, /*index=5*/f32[6,128]{1,0:T(8,128)}) custom-call(f32[768,128]{1,0:T(8,128)} %bitcast.12, f32[1536,128]{1,0:T(8,128)} %bitcast.11, bf16[27,128]{1,0:T(8,128)(2,1)} %wc.1, f32[1,128]{1,0:T(1,128)} %bitcast.14, ...), custom_call_target="tpu_custom_call" | custom-call | tf_op jit(solution)/shard_map/pallas_call | solution.py:603
  34.0 1.8 %shard_map.137 = (f32[768,128]{1,0:T(8,128)}, f32[27,128]{1,0:T(8,128)}, f32[1,128]{1,0:T(1,128)}, f32[128,128]{1,0:T(8,128)}, f32[1,128]{1,0:T(1,128)}, /*index=5*/f32[6,128]{1,0:T(8,128)}) custom-call(f32[768,128]{1,0:T(8,128)} %get-tuple-element.18.refs_0_, f32[27,128]{1,0:T(8,128)} %get-tuple-element.19.refs_1_, f32[1,128]{1,0:T(1,128)} %get-tuple-element.20.refs_2_, ...), custom_call_target="tpu_custom_call" | custom-call | tf_op jit(solution)/shard_map/pallas_call | solution.py:651
